TPU v7x, 768 devices: a whole 4x8x12 slice. The times are simulated.
768 devices in a mesh: section: 16 (over y_hi, x, core), fsdp: 48 (over z, y_lo).
Axes of the slice: x: 4, y: 8 (y_hi: 2, y_lo: 4; y = y_hi * 4 + y_lo), z: 12, core: 2. Of those that a mesh axis runs over, the one named last changes fastest.
Arguments:
- saved_input: bfloat16 [16, 2, 256, 6144], P('section', None, None, 'fsdp'), may hold values from -6 to 6
- incoming: bfloat16 [16, 256, 6144], P('section', None, 'fsdp'), may hold values from -6 to 6
- earlier_grad: bfloat16 [16, 256, 6144], P('section', None, 'fsdp'), may hold values from -6 to 6
- w_out: bfloat16 [16, 6144, 6144], P('section', 'fsdp'), may hold values from -0.078125 to 0.078125
- kernel: float32 [16, 3, 6144], P('section', None, 'fsdp'), may hold values from -3.5 to 3.5
- dilation: int32 [16], P('section'), may hold values from 1 to 64
Outputs:
- grad_input: bfloat16 [16, 256, 6144], P('section', None, 'fsdp')
- grad_kernel: float32 [16, 3, 6144], P('section', None, 'fsdp')
- grad_w_out: bfloat16 [16, 6144, 6144], P('section', 'fsdp')
All inputs are finite; a program needn't handle non-finite values.
Results may differ from a plain program's by a relative error of at most 0.0049.
Values may be sent and summed in bfloat16 or wider, within the bound.
No kernel may reach another device: no remote copies, remote signals or barrier semaphores. Data moves between devices by JAX's collectives and lax.ppermute only.
A program may use at most 32 MiB of HBM per device.

v0:
```python
import jax
import jax.numpy as jnp
from jax import lax
from jax.sharding import PartitionSpec as P

TAPS = 3


def from_behind(block, axis, distance):
    devices = range(lax.axis_size(axis))
    route = [((i - distance) % len(devices), i) for i in devices]
    return lax.ppermute(block, axis, route)


def delayed(values, offset):
    length = values.shape[-2]
    padded = jnp.concatenate([jnp.zeros_like(values), values], axis=-2)
    return lax.dynamic_slice_in_dim(padded, length - offset, length, values.ndim - 2)


def advanced(values, offset):
    length = values.shape[-2]
    padded = jnp.concatenate([values, jnp.zeros_like(values)], axis=-2)
    return lax.dynamic_slice_in_dim(padded, offset, length, values.ndim - 2)


def rows_by_cols(left, right):
    return lax.dot_general(
        left, right, (((1,), (1,)), ((), ())), preferred_element_type=jnp.float32
    )


def steps_by_steps(left, right):
    return lax.dot_general(
        left, right, (((0,), (0,)), ((), ())), preferred_element_type=jnp.float32
    )


def per_device(saved_input, incoming, earlier_grad, w_out, kernel, dilation):
    spacing = dilation[0]
    weight = w_out[0]
    taps_table = kernel[0]
    inputs = saved_input[0].astype(jnp.float32)
    conv = jnp.zeros(inputs.shape, jnp.float32)
    for tap in range(TAPS):
        conv = conv + taps_table[tap] * delayed(inputs, tap * spacing)
    hidden = conv.astype(jnp.bfloat16)
    earlier_rows = hidden[1]
    earlier_term = steps_by_steps(
        earlier_rows, lax.all_gather(earlier_grad, "fsdp", axis=2, tiled=True)[0]
    )
    shard_grad = from_behind(incoming, "section", -1)
    own_grad = shard_grad[0]
    whole = lax.all_gather(shard_grad, "fsdp", axis=2, tiled=True)
    back = rows_by_cols(whole[0], weight)
    grad_weight = earlier_term + steps_by_steps(hidden[0], whole[0])
    adjoint = own_grad.astype(jnp.float32)
    for tap in range(TAPS):
        adjoint = adjoint + taps_table[tap] * advanced(back, tap * spacing)
    grad_input = adjoint.astype(jnp.bfloat16)
    grad_kernel = jnp.stack(
        [jnp.sum(back * delayed(inputs[0], tap * spacing), axis=0) for tap in range(TAPS)]
    )
    return (grad_input[None], grad_kernel[None], grad_weight.astype(jnp.bfloat16)[None])


def solution(mesh):
    return jax.shard_map(
        per_device,
        mesh=mesh,
        in_specs=(
            P("section", None, None, "fsdp"),
            P("section", None, "fsdp"),
            P("section", None, "fsdp"),
            P("section", "fsdp", None),
            P("section", None, "fsdp"),
            P("section"),
        ),
        out_specs=(
            P("section", None, "fsdp"),
            P("section", None, "fsdp"),
            P("section", "fsdp", None),
        ),
        check_vma=False,
    )
```

profile of v0, /device:TPU:6, one launch (start us, length us, event | category | flops | bytes accessed | tf_op | source)
XLA Modules:
  0.0 436.2 jit_solution(7605820460635220315)
XLA Ops:
  7.2 0.0 copy-start
  7.2 0.0 all-gather.5.cloned.1.call-start
  7.2 0.7 all-gather.5.cloned.1.call-update
  7.9 0.0 all-gather.3.cloned.1.call-start
  8.0 2.2 collective-permute-start
  10.1 2.2 collective-permute-done
  12.3 0.0 copy-start.2
  12.3 0.6 copy-done.2
  13.0 0.0 all-gather.3.cloned.1.call-update
  13.7 0.7 slice_bitcast_fusion.7
  14.4 0.9 convert_bitcast_fusion
  15.3 0.1 fusion.11
  15.5 204.4 %all-gather.5.cloned.1.call-done = bf16[1,256,6144]{2,1,0:T(8,128)(2,1)} async-done(((bf16[1,256,128]{2,1,0:T(8,128)(2,1)}), bf16[1,256,6144]{2,1,0:T(8,128)(2,1)}) %all-gather.5.cloned.1.call-update) | async-done | bytes 3145744 | tf_op jit(solution)/shard_map/all_gather | solution.py:50
  219.8 4.2 fusion.2
  224.0 0.0 copy-start.3
  224.0 197.1 %all-gather.3.cloned.1.call-done = bf16[1,256,6144]{2,1,0:T(8,128)(2,1)} async-done(((bf16[1,256,128]{2,1,0:T(8,128)(2,1)}), bf16[1,256,6144]{2,1,0:T(8,128)(2,1)}) %all-gather.3.cloned.1.call-update) | async-done | bytes 3145744 | tf_op jit(solution)/shard_map/all_gather | solution.py:54
  421.1 0.0 copy-done
  421.1 0.0 copy-start.1
  421.1 3.0 fusion.5
  424.1 0.0 copy-done.3
  424.1 0.9 fusion.19
  425.0 0.6 copy.9
  425.6 0.0 copy-done.1
  425.6 3.7 fusion.1
  (2 shorter events, 0.0 us)
Async XLA Ops:
  7.2 413.9 %copy-start = (bf16[1,128,6144]{2,1,0:T(8,128)(2,1)S(1)}, bf16[1,128,6144]{2,1,0:T(8,128)(2,1)}, u32[]{:S(2)}) copy-start(bf16[1,128,6144]{2,1,0:T(8,128)(2,1)} %param.9) | copy-start | bytes 4718596
  7.2 212.7 %all-gather.5.cloned.1.call-start = ((), (), s32[]{:S(2)}) async-start(), calls=%async_computation.1 | async-start | bytes 3211264 | tf_op jit(solution)/shard_map/all_gather | solution.py:50
  7.9 413.2 %all-gather.3.cloned.1.call-start = ((), (), s32[]{:S(2)}) async-start(), calls=%async_computation | async-start | bytes 3211264 | tf_op jit(solution)/shard_map/all_gather | solution.py:54
  8.0 4.4 %collective-permute-start = (bf16[1,256,128]{2,1,0:T(8,128)(2,1)}, bf16[1,256,128]{2,1,0:T(8,128)(2,1)S(1)}, u32[]{:S(2)}, u32[]{:S(2)}) collective-permute-start(bf16[1,256,128]{2,1,0:T(8,128)(2,1)} %param.7), channel_id=1, source_target_pairs={{48,0},{96,48},{144,96},{192,144},{240,192},{288,240},{336,288},{3... | collective-permute-start | bytes 196616 | tf_op jit(solution)/shard_map/ppermute | solution.py:12
  12.3 0.6 copy-start.2
  224.0 200.1 %copy-start.3 = (bf16[1,256,128]{2,1,0:T(8,128)(2,1)S(1)}, bf16[1,256,128]{2,1,0:T(8,128)(2,1)}, u32[]{:S(2)}) copy-start(bf16[1,256,128]{2,1,0:T(8,128)(2,1)} %copy-done.2) | copy-start | bytes 196612
  421.1 4.5 %copy-start.1 = (bf16[1,256,6144]{2,1,0:T(8,128)(2,1)S(1)}, bf16[1,256,6144]{2,1,0:T(8,128)(2,1)}, u32[]{:S(2)}) copy-start(bf16[1,256,6144]{2,1,0:T(8,128)(2,1)} %all-gather.3.cloned.1.call-done) | copy-start | bytes 9437188
Sparse Core Ops, SparseCore 0:
  10.3 209.4 all-gather.4
  222.7 198.3 all-gather.2
where the time goes:
time: 437 us; the launch traced here: 436 us
  waiting for transfers between devices  404 us (92%)
  between operations  14.8 us (3%)
  matrix products  10.9 us (2%)
    all_gather x1, waiting for transfers between devices, per_device(): lax.all_gather(earlier_grad, 'fsdp', axis=2, tiled=True)[0]  204 us
    all_gather x1, waiting for transfers between devices, per_device(): whole = lax.all_gather(shard_grad, 'fsdp', axis=2, tiled=True)  197 us
  transfers between devices with their start and end apart: 3, of which 3 were waited for; matrix products, arithmetic and copies ran while one was open for 1% of the time, Pallas kernels for 0%

commit v1 on v0

v1 whole, which is shorter than its diff:
```python
import functools

import jax
import jax.numpy as jnp
from jax import lax
from jax.experimental import pallas as pl
from jax.experimental.pallas import tpu as pltpu
from jax.sharding import PartitionSpec as P

TAPS = 3
SECTIONS = 16
NZ = 12
NY = 4
SEQ = 256
LANES = 128
VMEM_LIMIT = 48 * 1024 * 1024

BATCHES = ((0, -1, 1, -2, 2, -3, 3), (-4, 4, -5, 5, -6))


def along(block, move):
    route = []
    for i in range(NZ * NY):
        z, y = move(i // NY, i % NY)
        route.append((i, (z % NZ) * NY + y))
    return lax.ppermute(block, "fsdp", route)


def from_next_section(block, flip):
    total = NZ * NY
    route = []
    for s in range(SECTIONS):
        for i in range(total):
            source = ((s + 1) % SECTIONS) * total + (i ^ flip)
            route.append((source, s * total + i))
    return lax.ppermute(block, ("section", "fsdp"), route)


def delayed(values, offset):
    rows = lax.broadcasted_iota(jnp.int32, values.shape, 0)
    return jnp.where(rows >= offset, pltpu.roll(values, offset, 0), 0.0)


def advanced(values, offset):
    length = values.shape[0]
    rows = lax.broadcasted_iota(jnp.int32, values.shape, 0)
    shifted = pltpu.roll(values, lax.rem(length - offset, length), 0)
    return jnp.where(rows < length - offset, shifted, 0.0)


def hidden_kernel(spacing_ref, saved_ref, taps_ref, out_ref):
    spacing = spacing_ref[0]
    for slot, batch in ((0, 1), (1, 0)):
        values = saved_ref[batch].astype(jnp.float32)
        conv = taps_ref[0:1, :] * values
        for tap in range(1, TAPS):
            conv = conv + taps_ref[tap : tap + 1, :] * delayed(values, tap * spacing)
        out_ref[:, slot * SEQ : (slot + 1) * SEQ] = conv.T.astype(jnp.bfloat16)


def hidden_rows(saved, taps, spacing):
    return pl.pallas_call(
        hidden_kernel,
        out_shape=jax.ShapeDtypeStruct((LANES, 2 * SEQ), jnp.bfloat16),
        in_specs=[
            pl.BlockSpec(memory_space=pltpu.SMEM),
            pl.BlockSpec(memory_space=pltpu.VMEM),
            pl.BlockSpec(memory_space=pltpu.VMEM),
        ],
        out_specs=pl.BlockSpec(memory_space=pltpu.VMEM),
        compiler_params=pltpu.CompilerParams(vmem_limit_bytes=VMEM_LIMIT),
        name="hidden",
    )(spacing, saved, taps)


def split_kernel(place_ref, weight_ref, keep_ref, send_ref):
    y = place_ref[1]
    for z in range(weight_ref.shape[1] // (NY * LANES)):
        for slot, flip in ((0, 0), (1, 2)):
            for target, other in ((keep_ref, 0), (send_ref, 1)):
                column = (z * NY + (y ^ (flip + other))) * LANES
                target[slot, z] = weight_ref[:, pl.ds(pl.multiple_of(column, LANES), LANES)]


def split_weight(place, weight):
    steps, per = 3, NZ // 3
    out = jax.ShapeDtypeStruct((2, NZ, LANES, LANES), jnp.bfloat16)
    block = pl.BlockSpec((2, per, LANES, LANES), lambda i: (0, i, 0, 0))
    return pl.pallas_call(
        split_kernel,
        out_shape=(out, out),
        grid=(steps,),
        in_specs=[
            pl.BlockSpec(memory_space=pltpu.SMEM),
            pl.BlockSpec((LANES, per * NY * LANES), lambda i: (0, i)),
        ],
        out_specs=(block, block),
        compiler_params=pltpu.CompilerParams(vmem_limit_bytes=VMEM_LIMIT),
        name="split_weight",
    )(place, weight)


def partial_kernel(slot, places, place_ref, own_ref, partner_ref, keep_ref, got_ref, *refs):
    count = len(places)
    blocks = refs[:count] if count > 1 else [refs[0]]
    refs = refs[len(blocks) :]
    had_refs, (mine_ref, theirs_ref, back_mine_ref, back_theirs_ref) = refs[:-4], refs[-4:]
    left = jnp.concatenate([own_ref[...], partner_ref[...]], axis=0)
    if had_refs:
        back = jnp.concatenate([had_refs[0][...], had_refs[1][...]], axis=1)
    else:
        back = jnp.zeros((SEQ, 2 * LANES), jnp.float32)
    for i, place in enumerate(places):
        block = blocks[i][...]
        grad = jnp.dot(left, block, preferred_element_type=jnp.float32)
        mine_ref[i] = grad[:LANES].astype(jnp.bfloat16)
        theirs_ref[i] = grad[LANES:].astype(jnp.bfloat16)
        at = lax.rem(place_ref[0] + (place + NZ), NZ)
        weight = jnp.concatenate([keep_ref[slot, at], got_ref[slot, at]], axis=0)
        back = back + lax.dot_general(
            block[SEQ:], weight, (((1,), (1,)), ((), ())), preferred_element_type=jnp.float32
        )
    back_mine_ref[...] = back[:, :LANES]
    back_theirs_ref[...] = back[:, LANES:]


def gathered_kernel(place_ref, own_ref, partner_ref, keep_ref, got_ref, all_ref, had_mine, had_theirs, mine_ref, theirs_ref, back_mine_ref, back_theirs_ref):
    left = jnp.concatenate([own_ref[...], partner_ref[...]], axis=0)
    back = jnp.concatenate([had_mine[...], had_theirs[...]], axis=1)
    for z in range(NZ):
        block = all_ref[z]
        grad = jnp.dot(left, block, preferred_element_type=jnp.float32)
        mine_ref[z] = grad[:LANES].astype(jnp.bfloat16)
        theirs_ref[z] = grad[LANES:].astype(jnp.bfloat16)
        weight = jnp.concatenate([keep_ref[0, z], got_ref[0, z]], axis=0)
        back = back + lax.dot_general(
            block[SEQ:], weight, (((1,), (1,)), ((), ())), preferred_element_type=jnp.float32
        )
    back_mine_ref[...] = back[:, :LANES]
    back_theirs_ref[...] = back[:, LANES:]


def products(kernel, name, count, operands):
    grads = jax.ShapeDtypeStruct((count, LANES, LANES), jnp.bfloat16)
    backs = jax.ShapeDtypeStruct((SEQ, LANES), jnp.float32)
    flops = 2 * count * (2 * LANES * 2 * SEQ * LANES + SEQ * 2 * LANES * LANES)
    whole = pl.BlockSpec(memory_space=pltpu.VMEM)
    return pl.pallas_call(
        kernel,
        out_shape=(grads, grads, backs, backs),
        in_specs=[pl.BlockSpec(memory_space=pltpu.SMEM)] + [whole] * (len(operands) - 1),
        out_specs=(whole,) * 4,
        compiler_params=pltpu.CompilerParams(vmem_limit_bytes=VMEM_LIMIT),
        cost_estimate=pl.CostEstimate(flops=flops, bytes_accessed=1 << 20, transcendentals=0),
        name=name,
    )(*operands)


def adjoint_kernel(spacing_ref, received_ref, saved_ref, taps_ref, mine_ref, theirs_ref, input_ref, taps_out_ref):
    spacing = spacing_ref[0]
    back = mine_ref[...] + theirs_ref[...]
    values = saved_ref[0].astype(jnp.float32)
    total = received_ref[...].astype(jnp.float32)
    for tap in range(TAPS):
        offset = tap * spacing
        total = total + taps_ref[tap : tap + 1, :] * advanced(back, offset)
        taps_out_ref[tap : tap + 1, :] = jnp.sum(back * delayed(values, offset), axis=0, keepdims=True)
    input_ref[...] = total.astype(jnp.bfloat16)


def adjoint(spacing, received, saved, taps, mine, theirs):
    whole = pl.BlockSpec(memory_space=pltpu.VMEM)
    return pl.pallas_call(
        adjoint_kernel,
        out_shape=(
            jax.ShapeDtypeStruct((SEQ, LANES), jnp.bfloat16),
            jax.ShapeDtypeStruct((TAPS, LANES), jnp.float32),
        ),
        in_specs=[pl.BlockSpec(memory_space=pltpu.SMEM)] + [whole] * 5,
        out_specs=(whole, whole),
        compiler_params=pltpu.CompilerParams(vmem_limit_bytes=VMEM_LIMIT),
        name="adjoint",
    )(spacing, received, saved, taps, mine, theirs)


def assemble_kernel(place_ref, own_all_ref, got_all_ref, *refs):
    out_ref, refs = refs[-1], refs[:-1]
    z, y = place_ref[0], place_ref[1]
    for at in range(NZ):
        for flip, source in ((0, own_all_ref), (1, got_all_ref)):
            column = (at * NY + (y ^ flip)) * LANES
            out_ref[:, pl.ds(pl.multiple_of(column, LANES), LANES)] = source[at]
    for number, places in enumerate(BATCHES):
        for i, place in enumerate(places):
            at = lax.rem(z + (place + NZ), NZ)
            for flip, source in ((2, refs[2 * number]), (3, refs[2 * number + 1])):
                column = (at * NY + (y ^ flip)) * LANES
                out_ref[:, pl.ds(pl.multiple_of(column, LANES), LANES)] = source[i]


def assemble(place, own_all, got_all, pieces):
    whole = pl.BlockSpec(memory_space=pltpu.VMEM)
    return pl.pallas_call(
        assemble_kernel,
        out_shape=jax.ShapeDtypeStruct((LANES, NZ * NY * LANES), jnp.bfloat16),
        in_specs=[pl.BlockSpec(memory_space=pltpu.SMEM)] + [whole] * (2 + len(pieces)),
        out_specs=whole,
        compiler_params=pltpu.CompilerParams(vmem_limit_bytes=VMEM_LIMIT),
        name="assemble",
    )(place, own_all, got_all, *pieces)


def per_device(saved_input, incoming, earlier_grad, w_out, kernel, dilation):
    saved, taps, weight = saved_input[0], kernel[0], w_out[0]
    earlier = earlier_grad[0]
    index = lax.axis_index("fsdp")
    place = jnp.stack([index // NY, index % NY]).astype(jnp.int32)
    partner = lambda z, y: (z, y ^ 1)

    received = from_next_section(incoming[0], 0)
    received_other = from_next_section(incoming[0], 2)
    earlier_other = along(earlier, lambda z, y: (z, y ^ 2))
    own_block = jnp.concatenate([earlier, received], axis=0)
    groups = [[z * NY + y for z in range(NZ)] for y in range(NY)]
    gathered = lax.all_gather(own_block, "fsdp", axis=0, axis_index_groups=groups)

    ring = {0: jnp.concatenate([earlier_other, received_other], axis=0)}
    for step in range(1, NZ // 2 + 1):
        ring[-step] = along(ring[1 - step], lambda z, y: (z + 1, y))
        if step < NZ // 2:
            ring[step] = along(ring[step - 1], lambda z, y: (z - 1, y))

    rows = hidden_rows(saved, taps, dilation)
    rows_partner = along(rows, partner)
    keep, send = split_weight(place, weight)
    got = along(send, partner)

    backs, pieces = (), []
    for places in BATCHES:
        mine, theirs, *backs = products(
            functools.partial(partial_kernel, 1, places),
            "ring_products",
            len(places),
            (place, rows, rows_partner, keep, got, *(ring[p] for p in places), *backs),
        )
        pieces += [mine, along(theirs, partner)]
    own_all, theirs_all, back_mine, back_theirs = products(
        gathered_kernel, "gathered_products", NZ, (place, rows, rows_partner, keep, got, gathered, *backs)
    )
    back_other = along(back_theirs, partner)
    got_all = along(theirs_all, partner)
    grad_input, grad_kernel = adjoint(dilation, received, saved, taps, back_mine, back_other)
    grad_weight = assemble(place, own_all, got_all, pieces)
    return grad_input[None], grad_kernel[None], grad_weight[None]


def solution(mesh):
    return jax.shard_map(
        per_device,
        mesh=mesh,
        in_specs=(
            P("section", None, None, "fsdp"),
            P("section", None, "fsdp"),
            P("section", None, "fsdp"),
            P("section", "fsdp", None),
            P("section", None, "fsdp"),
            P("section"),
        ),
        out_specs=(
            P("section", None, "fsdp"),
            P("section", None, "fsdp"),
            P("section", "fsdp", None),
        ),
        check_vma=False,
    )
```

time: 437 us -> 138 us (0.32)
  the two profiles are of different devices: /device:TPU:6 before, /device:TPU:8 now
where the time goes in v1:
time: 138 us; the launch traced here: 137 us
  starting transfers between devices  85.5 us (62%)
  waiting for transfers between devices  22.2 us (16%)
  between operations  15.1 us (11%)
  Pallas kernels  9 us (7%)
  local copies, waits for them, and re-layouts  3.4 us (2%)
  other arithmetic  1.58 us (1%)
    ppermute x18, starting transfers between devices, along(): return lax.ppermute(block, 'fsdp', route)  68.1 us
    ppermute x18, waiting for transfers between devices, along(): return lax.ppermute(block, 'fsdp', route)  19.8 us
    ppermute x2, starting transfers between devices, from_next_section(): return lax.ppermute(block, ('section', 'fsdp'), route)  17.4 us
    pallas_call x3, Pallas kernels, products(): pl.pallas_call(kernel, out_shape=(grads, grads, backs, backs), in_specs=[...  4.55 us
    unnamed x11, local copies, waits for them, and re-layouts  3.39 us
  transfers between devices with their start and end apart: 21, of which 7 were waited for; matrix products, arithmetic and copies ran while one was open for 0% of the time, Pallas kernels for 4%

profile of v1, /device:TPU:8, one launch (start us, length us, event | category | flops | bytes accessed | tf_op | source)
XLA Modules:
  0.0 136.8 jit_solution(4780470170792397362)
XLA Ops:
  7.2 0.0 all-gather.3.cloned.1.call-start
  7.2 8.6 %collective-permute-start = (bf16[256,128]{1,0:T(8,128)(2,1)}, bf16[256,128]{1,0:T(8,128)(2,1)S(1)}, u32[]{:S(2)}, u32[]{:S(2)}) collective-permute-start(bf16[256,128]{1,0:T(8,128)(2,1)} %bitcast.23), channel_id=1, source_target_pairs={{48,0},{49,1},{50,2},{51,3},{52,4},{53,5},{54,6},{55,7},{56,8},{57... | collective-permute-start | bytes 196616 | tf_op jit(solution)/shard_map/ppermute | solution.py:36
  15.8 2.4 %collective-permute-done.received_ref = bf16[256,128]{1,0:T(8,128)(2,1)S(1)} collective-permute-done((bf16[256,128]{1,0:T(8,128)(2,1)}, bf16[256,128]{1,0:T(8,128)(2,1)S(1)}, u32[]{:S(2)}, u32[]{:S(2)}) %collective-permute-start) | collective-permute-done | bytes 65568 | tf_op jit(solution)/shard_map/ppermute | solution.py:36
  18.3 1.5 %pad_maximum_fusion = bf16[512,128]{1,0:T(8,128)(2,1)} fusion(bf16[256,128]{1,0:T(8,128)(2,1)S(1)} %collective-permute-done.received_ref, bf16[256,128]{1,0:T(8,128)(2,1)} %bitcast.21), kind=kLoop, calls=%fused_computation | loop fusion | flops 262144 | bytes 262144 | tf_op jit(solution)/shard_map/concatenate | solution.py:223
  19.8 0.0 all-gather.3.cloned.1.call-update
  19.8 3.1 %collective-permute-start.3 = (bf16[256,128]{1,0:T(8,128)(2,1)}, bf16[256,128]{1,0:T(8,128)(2,1)S(1)}, u32[]{:S(2)}, u32[]{:S(2)}) collective-permute-start(bf16[256,128]{1,0:T(8,128)(2,1)} %bitcast.22), channel_id=1, source_target_pairs={{0,2},{1,3},{2,0},{3,1},{4,6},{5,7},{6,4},{7,5},{8,10},{9,11},{10,... | collective-permute-start | bytes 196616 | tf_op jit(solution)/shard_map/ppermute | solution.py:26
  22.9 8.8 %collective-permute-start.4 = (bf16[256,128]{1,0:T(8,128)(2,1)}, bf16[256,128]{1,0:T(8,128)(2,1)S(1)}, u32[]{:S(2)}, u32[]{:S(2)}) collective-permute-start(bf16[256,128]{1,0:T(8,128)(2,1)} %bitcast.24), channel_id=1, source_target_pairs={{50,0},{51,1},{48,2},{49,3},{54,4},{55,5},{52,6},{53,7},{58,8},{59... | collective-permute-start | bytes 196616 | tf_op jit(solution)/shard_map/ppermute | solution.py:36
  31.7 0.1 pad_add_fusion.place_ref
  31.8 1.4 %copy-done = bf16[1,128,6144]{2,1,0:T(8,128)(2,1)S(1)} copy-done((bf16[1,128,6144]{2,1,0:T(8,128)(2,1)S(1)}, bf16[1,128,6144]{2,1,0:T(8,128)(2,1)}, u32[]{:S(2)}) %copy-start) | copy-done | bytes 1572888
  33.2 1.2 split_weight.1
  34.4 4.6 %collective-permute-start.2 = (bf16[2,12,128,128]{3,2,1,0:T(8,128)(2,1)S(1)}, bf16[2,12,128,128]{3,2,1,0:T(8,128)(2,1)S(1)}, u32[]{:S(2)}, u32[]{:S(2)}) collective-permute-start(bf16[2,12,128,128]{3,2,1,0:T(8,128)(2,1)S(1)} %get-tuple-element.20), channel_id=1, source_target_pairs={{0,1},{1,0},{2,3},{3,2},{4,5},{5,4},{6,7},{7,6},{8,9},{9,8},{10,11... | collective-permute-start | bytes 2359304 | tf_op jit(solution)/shard_map/ppermute | solution.py:26
  39.0 0.0 collective-permute-done.3
  39.1 0.0 collective-permute-done.4
  39.1 3.3 %collective-permute-start.5 = (bf16[512,128]{1,0:T(8,128)(2,1)S(1)}, bf16[512,128]{1,0:T(8,128)(2,1)S(1)}, u32[]{:S(2)}, u32[]{:S(2)}) collective-permute-start(bf16[512,128]{1,0:T(8,128)(2,1)S(1)} %constant_dynamic-update-slice_fusion.refs_0_), channel_id=1, source_target_pairs={{0,4},{1,5},{2,6},{3,7},{4,8},{5,9},{6,10},{7,11},{8,12},{9,13},{1... | collective-permute-start | bytes 393224 | tf_op jit(solution)/shard_map/ppermute | solution.py:26
  42.4 12.2 %collective-permute-start.9 = (bf16[512,128]{1,0:T(8,128)(2,1)S(1)}, bf16[512,128]{1,0:T(8,128)(2,1)S(1)}, u32[]{:S(2)}, u32[]{:S(2)}) collective-permute-start(bf16[512,128]{1,0:T(8,128)(2,1)S(1)} %constant_dynamic-update-slice_fusion.refs_0_), channel_id=1, source_target_pairs={{0,44},{1,45},{2,46},{3,47},{4,0},{5,1},{6,2},{7,3},{8,4},{9,5},{1... | collective-permute-start | bytes 393224 | tf_op jit(solution)/shard_map/ppermute | solution.py:26
  54.6 1.5 %collective-permute-done.5.refs_1_ = bf16[512,128]{1,0:T(8,128)(2,1)S(1)} collective-permute-done((bf16[512,128]{1,0:T(8,128)(2,1)S(1)}, bf16[512,128]{1,0:T(8,128)(2,1)S(1)}, u32[]{:S(2)}, u32[]{:S(2)}) %collective-permute-start.5) | collective-permute-done | bytes 131104 | tf_op jit(solution)/shard_map/ppermute | solution.py:26
  56.2 1.9 %collective-permute-start.6 = (bf16[512,128]{1,0:T(8,128)(2,1)S(1)}, bf16[512,128]{1,0:T(8,128)(2,1)S(1)}, u32[]{:S(2)}, u32[]{:S(2)}) collective-permute-start(bf16[512,128]{1,0:T(8,128)(2,1)S(1)} %collective-permute-done.5.refs_1_), channel_id=1, source_target_pairs={{0,4},{1,5},{2,6},{3,7},{4,8},{5,9},{6,10},{7,11},{8,12},{9,13},{1... | collective-permute-start | bytes 393224 | tf_op jit(solution)/shard_map/ppermute | solution.py:26
  58.1 0.0 collective-permute-done.9.refs_2_
  58.1 5.5 %collective-permute-start.10 = (bf16[512,128]{1,0:T(8,128)(2,1)S(1)}, bf16[512,128]{1,0:T(8,128)(2,1)S(1)}, u32[]{:S(2)}, u32[]{:S(2)}) collective-permute-start(bf16[512,128]{1,0:T(8,128)(2,1)S(1)} %collective-permute-done.9.refs_2_), channel_id=1, source_target_pairs={{0,44},{1,45},{2,46},{3,47},{4,0},{5,1},{6,2},{7,3},{8,4},{9,5},{1... | collective-permute-start | bytes 393224 | tf_op jit(solution)/shard_map/ppermute | solution.py:26
  63.6 1.9 %collective-permute-done.6.refs_3_ = bf16[512,128]{1,0:T(8,128)(2,1)S(1)} collective-permute-done((bf16[512,128]{1,0:T(8,128)(2,1)S(1)}, bf16[512,128]{1,0:T(8,128)(2,1)S(1)}, u32[]{:S(2)}, u32[]{:S(2)}) %collective-permute-start.6) | collective-permute-done | bytes 131104 | tf_op jit(solution)/shard_map/ppermute | solution.py:26
  65.5 1.9 %collective-permute-start.7 = (bf16[512,128]{1,0:T(8,128)(2,1)S(1)}, bf16[512,128]{1,0:T(8,128)(2,1)S(1)}, u32[]{:S(2)}, u32[]{:S(2)}) collective-permute-start(bf16[512,128]{1,0:T(8,128)(2,1)S(1)} %collective-permute-done.6.refs_3_), channel_id=1, source_target_pairs={{0,4},{1,5},{2,6},{3,7},{4,8},{5,9},{6,10},{7,11},{8,12},{9,13},{1... | collective-permute-start | bytes 393224 | tf_op jit(solution)/shard_map/ppermute | solution.py:26
  67.4 5.8 %collective-permute-start.11 = (bf16[512,128]{1,0:T(8,128)(2,1)S(1)}, bf16[512,128]{1,0:T(8,128)(2,1)S(1)}, u32[]{:S(2)}, u32[]{:S(2)}) collective-permute-start(bf16[512,128]{1,0:T(8,128)(2,1)S(1)} %collective-permute-done.10.refs_4_), channel_id=1, source_target_pairs={{0,44},{1,45},{2,46},{3,47},{4,0},{5,1},{6,2},{7,3},{8,4},{9,5},{1... | collective-permute-start | bytes 393224 | tf_op jit(solution)/shard_map/ppermute | solution.py:26
  73.2 4.4 %collective-permute-done.7.refs_5_ = bf16[512,128]{1,0:T(8,128)(2,1)S(1)} collective-permute-done((bf16[512,128]{1,0:T(8,128)(2,1)S(1)}, bf16[512,128]{1,0:T(8,128)(2,1)S(1)}, u32[]{:S(2)}, u32[]{:S(2)}) %collective-permute-start.7) | collective-permute-done | bytes 131104 | tf_op jit(solution)/shard_map/ppermute | solution.py:26
  77.6 1.9 %collective-permute-start.8 = (bf16[512,128]{1,0:T(8,128)(2,1)S(1)}, bf16[512,128]{1,0:T(8,128)(2,1)S(1)}, u32[]{:S(2)}, u32[]{:S(2)}) collective-permute-start(bf16[512,128]{1,0:T(8,128)(2,1)S(1)} %collective-permute-done.7.refs_5_), channel_id=1, source_target_pairs={{0,4},{1,5},{2,6},{3,7},{4,8},{5,9},{6,10},{7,11},{8,12},{9,13},{1... | collective-permute-start | bytes 393224 | tf_op jit(solution)/shard_map/ppermute | solution.py:26
  79.5 5.1 %collective-permute-start.12 = (bf16[512,128]{1,0:T(8,128)(2,1)S(1)}, bf16[512,128]{1,0:T(8,128)(2,1)S(1)}, u32[]{:S(2)}, u32[]{:S(2)}) collective-permute-start(bf16[512,128]{1,0:T(8,128)(2,1)S(1)} %collective-permute-done.11.refs_6_), channel_id=1, source_target_pairs={{0,44},{1,45},{2,46},{3,47},{4,0},{5,1},{6,2},{7,3},{8,4},{9,5},{1... | collective-permute-start | bytes 393224 | tf_op jit(solution)/shard_map/ppermute | solution.py:26
  84.7 2.4 %collective-permute-done.8.refs_0_ = bf16[512,128]{1,0:T(8,128)(2,1)S(1)} collective-permute-done((bf16[512,128]{1,0:T(8,128)(2,1)S(1)}, bf16[512,128]{1,0:T(8,128)(2,1)S(1)}, u32[]{:S(2)}, u32[]{:S(2)}) %collective-permute-start.8) | collective-permute-done | bytes 131104 | tf_op jit(solution)/shard_map/ppermute | solution.py:26
  87.1 1.9 %collective-permute-start.13 = (bf16[512,128]{1,0:T(8,128)(2,1)S(1)}, bf16[512,128]{1,0:T(8,128)(2,1)S(1)}, u32[]{:S(2)}, u32[]{:S(2)}) collective-permute-start(bf16[512,128]{1,0:T(8,128)(2,1)S(1)} %collective-permute-done.8.refs_0_), channel_id=1, source_target_pairs={{0,4},{1,5},{2,6},{3,7},{4,8},{5,9},{6,10},{7,11},{8,12},{9,13},{1... | collective-permute-start | bytes 393224 | tf_op jit(solution)/shard_map/ppermute | solution.py:26
  89.7 0.3 hidden.1.own_ref
  90.0 2.0 %collective-permute-start.1 = (bf16[128,512]{1,0:T(8,128)(2,1)S(1)}, bf16[128,512]{1,0:T(8,128)(2,1)S(1)}, u32[]{:S(2)}, u32[]{:S(2)}) collective-permute-start(bf16[128,512]{1,0:T(8,128)(2,1)S(1)} %hidden.1.own_ref), channel_id=1, source_target_pairs={{0,1},{1,0},{2,3},{3,2},{4,5},{5,4},{6,7},{7,6},{8,9},{9,8},{10,11... | collective-permute-start | bytes 393224 | tf_op jit(solution)/shard_map/ppermute | solution.py:26
  92.1 5.1 %collective-permute-start.14 = (bf16[512,128]{1,0:T(8,128)(2,1)S(1)}, bf16[512,128]{1,0:T(8,128)(2,1)S(1)}, u32[]{:S(2)}, u32[]{:S(2)}) collective-permute-start(bf16[512,128]{1,0:T(8,128)(2,1)S(1)} %collective-permute-done.12.refs_1_), channel_id=1, source_target_pairs={{0,44},{1,45},{2,46},{3,47},{4,0},{5,1},{6,2},{7,3},{8,4},{9,5},{1... | collective-permute-start | bytes 393224 | tf_op jit(solution)/shard_map/ppermute | solution.py:26
  97.2 0.0 collective-permute-done.13.refs_2_
  97.2 1.9 %collective-permute-start.15 = (bf16[512,128]{1,0:T(8,128)(2,1)S(1)}, bf16[512,128]{1,0:T(8,128)(2,1)S(1)}, u32[]{:S(2)}, u32[]{:S(2)}) collective-permute-start(bf16[512,128]{1,0:T(8,128)(2,1)S(1)} %collective-permute-done.13.refs_2_), channel_id=1, source_target_pairs={{0,4},{1,5},{2,6},{3,7},{4,8},{5,9},{6,10},{7,11},{8,12},{9,13},{1... | collective-permute-start | bytes 393224 | tf_op jit(solution)/shard_map/ppermute | solution.py:26
  99.2 1.4 %ring_products.2 = (bf16[7,128,128]{2,1,0:T(8,128)(2,1)S(1)}, bf16[7,128,128]{2,1,0:T(8,128)(2,1)S(1)}, f32[256,128]{1,0:T(8,128)S(1)}, f32[256,128]{1,0:T(8,128)S(1)}) custom-call(s32[2]{0:T(128)S(1)} %pad_add_fusion.place_ref, bf16[128,512]{1,0:T(8,128)(2,1)S(1)} %hidden.1.own_ref, bf16[128,512]{1,0:T(8,128)(2,1)S(1)} %collective-permute-done.1.partner_ref, ...), custom_call_target="tpu_custom_call" | custom-call | flops 352321536 | bytes 1048576 | tf_op jit(solution)/shard_map/ring_products/pallas_call | solution.py:148
  100.6 4.7 %collective-permute-done.15.refs_4_ = bf16[512,128]{1,0:T(8,128)(2,1)S(1)} collective-permute-done((bf16[512,128]{1,0:T(8,128)(2,1)S(1)}, bf16[512,128]{1,0:T(8,128)(2,1)S(1)}, u32[]{:S(2)}, u32[]{:S(2)}) %collective-permute-start.15) | collective-permute-done | bytes 131104 | tf_op jit(solution)/shard_map/ppermute | solution.py:26
  105.3 1.2 ring_products.3
  106.5 0.0 all-gather.3.cloned.1.call-done
  106.5 1.4 %copy-done.1 = bf16[6144,128]{1,0:T(8,128)(2,1)S(1)} copy-done((bf16[6144,128]{1,0:T(8,128)(2,1)S(1)}, bf16[6144,128]{1,0:T(8,128)(2,1)}, u32[]{:S(2)}) %copy-start.1) | copy-done | bytes 1572888
  107.9 1.9 %gathered_products.1 = (bf16[12,128,128]{2,1,0:T(8,128)(2,1)S(1)}, bf16[12,128,128]{2,1,0:T(8,128)(2,1)S(1)}, f32[256,128]{1,0:T(8,128)S(1)}, f32[256,128]{1,0:T(8,128)S(1)}) custom-call(s32[2]{0:T(128)S(1)} %pad_add_fusion.place_ref, bf16[128,512]{1,0:T(8,128)(2,1)S(1)} %hidden.1.own_ref, bf16[128,512]{1,0:T(8,128)(2,1)S(1)} %collective-permute-done.1.partner_ref, ...), custom_call_target="tpu_custom_call" | custom-call | flops 603979776 | bytes 1048576 | tf_op jit(solution)/shard_map/gathered_products/pallas_call | solution.py:148
  109.9 3.8 %collective-permute-start.17 = (bf16[12,128,128]{2,1,0:T(8,128)(2,1)S(1)}, bf16[12,128,128]{2,1,0:T(8,128)(2,1)S(1)}, u32[]{:S(2)}, u32[]{:S(2)}) collective-permute-start(bf16[12,128,128]{2,1,0:T(8,128)(2,1)S(1)} %get-tuple-element.30), channel_id=1, source_target_pairs={{0,1},{1,0},{2,3},{3,2},{4,5},{5,4},{6,7},{7,6},{8,9},{9,8},{10,11... | collective-permute-start | bytes 1179656 | tf_op jit(solution)/shard_map/ppermute | solution.py:26
  113.7 2.0 %collective-permute-start.18 = (bf16[7,128,128]{2,1,0:T(8,128)(2,1)S(1)}, bf16[7,128,128]{2,1,0:T(8,128)(2,1)S(1)}, u32[]{:S(2)}, u32[]{:S(2)}) collective-permute-start(bf16[7,128,128]{2,1,0:T(8,128)(2,1)S(1)} %get-tuple-element.32), channel_id=1, source_target_pairs={{0,1},{1,0},{2,3},{3,2},{4,5},{5,4},{6,7},{7,6},{8,9},{9,8},{10,11... | collective-permute-start | bytes 688136 | tf_op jit(solution)/shard_map/ppermute | solution.py:26
  115.7 3.8 %collective-permute-start.19 = (bf16[5,128,128]{2,1,0:T(8,128)(2,1)S(1)}, bf16[5,128,128]{2,1,0:T(8,128)(2,1)S(1)}, u32[]{:S(2)}, u32[]{:S(2)}) collective-permute-start(bf16[5,128,128]{2,1,0:T(8,128)(2,1)S(1)} %get-tuple-element.34), channel_id=1, source_target_pairs={{0,1},{1,0},{2,3},{3,2},{4,5},{5,4},{6,7},{7,6},{8,9},{9,8},{10,11... | collective-permute-start | bytes 491528 | tf_op jit(solution)/shard_map/ppermute | solution.py:26
  119.6 2.0 %collective-permute-start.16 = (f32[256,128]{1,0:T(8,128)S(1)}, f32[256,128]{1,0:T(8,128)S(1)}, u32[]{:S(2)}, u32[]{:S(2)}) collective-permute-start(f32[256,128]{1,0:T(8,128)S(1)} %get-tuple-element.26), channel_id=1, source_target_pairs={{0,1},{1,0},{2,3},{3,2},{4,5},{5,4},{6,7},{7,6},{8,9},{9,8},{10,11... | collective-permute-start | bytes 393224 | tf_op jit(solution)/shard_map/ppermute | solution.py:26
  121.6 4.8 %collective-permute-done.16.theirs_ref = f32[256,128]{1,0:T(8,128)S(1)} collective-permute-done((f32[256,128]{1,0:T(8,128)S(1)}, f32[256,128]{1,0:T(8,128)S(1)}, u32[]{:S(2)}, u32[]{:S(2)}) %collective-permute-start.16) | collective-permute-done | bytes 131104 | tf_op jit(solution)/shard_map/ppermute | solution.py:26
  126.4 0.8 adjoint.1
  127.2 0.6 copy.9
  127.8 0.0 collective-permute-done.18.refs_1_
  127.8 0.0 collective-permute-done.17.got_all_ref
  127.8 2.1 %assemble.1 = bf16[128,6144]{1,0:T(8,128)(2,1)} custom-call(s32[2]{0:T(128)S(1)} %pad_add_fusion.place_ref, bf16[12,128,128]{2,1,0:T(8,128)(2,1)S(1)} %get-tuple-element.29.own_all_ref, bf16[12,128,128]{2,1,0:T(8,128)(2,1)S(1)} %collective-permute-done.17.got_all_ref, bf16[7,128,128]{2,1,0:T(8,128)(2,1)S(1)} %get-tuple-element.31.refs_0_, ...), custom_call_target="tpu_custom_call" | custom-call | tf_op jit(solution)/shard_map/assemble/pallas_call | solution.py:203
  (16 shorter events, 0.1 us)
Async XLA Ops:
  7.2 81.9 %copy-start.3 = (f32[1,3,128]{2,0,1:T(1,128)S(1)}, f32[1,3,128]{2,0,1:T(1,128)}, u32[]{:S(2)}) copy-start(f32[1,3,128]{2,0,1:T(1,128)} %param.10) | copy-start | bytes 4612
  7.2 82.5 %copy-start.2 = (bf16[1,2,256,128]{3,2,1,0:T(8,128)(2,1)S(1)}, bf16[1,2,256,128]{3,2,1,0:T(8,128)(2,1)}, u32[]{:S(2)}) copy-start(bf16[1,2,256,128]{3,2,1,0:T(8,128)(2,1)} %param.6) | copy-start | bytes 393220
  7.2 99.3 %all-gather.3.cloned.1.call-start = ((), (), s32[]{:S(2)}) async-start(), calls=%async_computation | async-start | bytes 1703936 | tf_op jit(solution)/shard_map/all_gather | solution.py:225
  7.2 11.0 %collective-permute-start = (bf16[256,128]{1,0:T(8,128)(2,1)}, bf16[256,128]{1,0:T(8,128)(2,1)S(1)}, u32[]{:S(2)}, u32[]{:S(2)}) collective-permute-start(bf16[256,128]{1,0:T(8,128)(2,1)} %bitcast.23), channel_id=1, source_target_pairs={{48,0},{49,1},{50,2},{51,3},{52,4},{53,5},{54,6},{55,7},{56,8},{57... | collective-permute-start | bytes 196616 | tf_op jit(solution)/shard_map/ppermute | solution.py:36
  19.8 19.3 %collective-permute-start.3 = (bf16[256,128]{1,0:T(8,128)(2,1)}, bf16[256,128]{1,0:T(8,128)(2,1)S(1)}, u32[]{:S(2)}, u32[]{:S(2)}) collective-permute-start(bf16[256,128]{1,0:T(8,128)(2,1)} %bitcast.22), channel_id=1, source_target_pairs={{0,2},{1,3},{2,0},{3,1},{4,6},{5,7},{6,4},{7,5},{8,10},{9,11},{10,... | collective-permute-start | bytes 196616 | tf_op jit(solution)/shard_map/ppermute | solution.py:26
  22.9 16.2 %collective-permute-start.4 = (bf16[256,128]{1,0:T(8,128)(2,1)}, bf16[256,128]{1,0:T(8,128)(2,1)S(1)}, u32[]{:S(2)}, u32[]{:S(2)}) collective-permute-start(bf16[256,128]{1,0:T(8,128)(2,1)} %bitcast.24), channel_id=1, source_target_pairs={{50,0},{51,1},{48,2},{49,3},{54,4},{55,5},{52,6},{53,7},{58,8},{59... | collective-permute-start | bytes 196616 | tf_op jit(solution)/shard_map/ppermute | solution.py:36
  31.8 1.4 %copy-start = (bf16[1,128,6144]{2,1,0:T(8,128)(2,1)S(1)}, bf16[1,128,6144]{2,1,0:T(8,128)(2,1)}, u32[]{:S(2)}) copy-start(bf16[1,128,6144]{2,1,0:T(8,128)(2,1)} %param.9) | copy-start | bytes 4718596
  34.4 64.7 %collective-permute-start.2 = (bf16[2,12,128,128]{3,2,1,0:T(8,128)(2,1)S(1)}, bf16[2,12,128,128]{3,2,1,0:T(8,128)(2,1)S(1)}, u32[]{:S(2)}, u32[]{:S(2)}) collective-permute-start(bf16[2,12,128,128]{3,2,1,0:T(8,128)(2,1)S(1)} %get-tuple-element.20), channel_id=1, source_target_pairs={{0,1},{1,0},{2,3},{3,2},{4,5},{5,4},{6,7},{7,6},{8,9},{9,8},{10,11... | collective-permute-start | bytes 2359304 | tf_op jit(solution)/shard_map/ppermute | solution.py:26
  39.1 17.1 %collective-permute-start.5 = (bf16[512,128]{1,0:T(8,128)(2,1)S(1)}, bf16[512,128]{1,0:T(8,128)(2,1)S(1)}, u32[]{:S(2)}, u32[]{:S(2)}) collective-permute-start(bf16[512,128]{1,0:T(8,128)(2,1)S(1)} %constant_dynamic-update-slice_fusion.refs_0_), channel_id=1, source_target_pairs={{0,4},{1,5},{2,6},{3,7},{4,8},{5,9},{6,10},{7,11},{8,12},{9,13},{1... | collective-permute-start | bytes 393224 | tf_op jit(solution)/shard_map/ppermute | solution.py:26
  42.4 15.7 %collective-permute-start.9 = (bf16[512,128]{1,0:T(8,128)(2,1)S(1)}, bf16[512,128]{1,0:T(8,128)(2,1)S(1)}, u32[]{:S(2)}, u32[]{:S(2)}) collective-permute-start(bf16[512,128]{1,0:T(8,128)(2,1)S(1)} %constant_dynamic-update-slice_fusion.refs_0_), channel_id=1, source_target_pairs={{0,44},{1,45},{2,46},{3,47},{4,0},{5,1},{6,2},{7,3},{8,4},{9,5},{1... | collective-permute-start | bytes 393224 | tf_op jit(solution)/shard_map/ppermute | solution.py:26
  56.2 9.3 %collective-permute-start.6 = (bf16[512,128]{1,0:T(8,128)(2,1)S(1)}, bf16[512,128]{1,0:T(8,128)(2,1)S(1)}, u32[]{:S(2)}, u32[]{:S(2)}) collective-permute-start(bf16[512,128]{1,0:T(8,128)(2,1)S(1)} %collective-permute-done.5.refs_1_), channel_id=1, source_target_pairs={{0,4},{1,5},{2,6},{3,7},{4,8},{5,9},{6,10},{7,11},{8,12},{9,13},{1... | collective-permute-start | bytes 393224 | tf_op jit(solution)/shard_map/ppermute | solution.py:26
  58.1 9.3 %collective-permute-start.10 = (bf16[512,128]{1,0:T(8,128)(2,1)S(1)}, bf16[512,128]{1,0:T(8,128)(2,1)S(1)}, u32[]{:S(2)}, u32[]{:S(2)}) collective-permute-start(bf16[512,128]{1,0:T(8,128)(2,1)S(1)} %collective-permute-done.9.refs_2_), channel_id=1, source_target_pairs={{0,44},{1,45},{2,46},{3,47},{4,0},{5,1},{6,2},{7,3},{8,4},{9,5},{1... | collective-permute-start | bytes 393224 | tf_op jit(solution)/shard_map/ppermute | solution.py:26
  65.5 12.1 %collective-permute-start.7 = (bf16[512,128]{1,0:T(8,128)(2,1)S(1)}, bf16[512,128]{1,0:T(8,128)(2,1)S(1)}, u32[]{:S(2)}, u32[]{:S(2)}) collective-permute-start(bf16[512,128]{1,0:T(8,128)(2,1)S(1)} %collective-permute-done.6.refs_3_), channel_id=1, source_target_pairs={{0,4},{1,5},{2,6},{3,7},{4,8},{5,9},{6,10},{7,11},{8,12},{9,13},{1... | collective-permute-start | bytes 393224 | tf_op jit(solution)/shard_map/ppermute | solution.py:26
  67.4 12.1 %collective-permute-start.11 = (bf16[512,128]{1,0:T(8,128)(2,1)S(1)}, bf16[512,128]{1,0:T(8,128)(2,1)S(1)}, u32[]{:S(2)}, u32[]{:S(2)}) collective-permute-start(bf16[512,128]{1,0:T(8,128)(2,1)S(1)} %collective-permute-done.10.refs_4_), channel_id=1, source_target_pairs={{0,44},{1,45},{2,46},{3,47},{4,0},{5,1},{6,2},{7,3},{8,4},{9,5},{1... | collective-permute-start | bytes 393224 | tf_op jit(solution)/shard_map/ppermute | solution.py:26
  77.6 9.5 %collective-permute-start.8 = (bf16[512,128]{1,0:T(8,128)(2,1)S(1)}, bf16[512,128]{1,0:T(8,128)(2,1)S(1)}, u32[]{:S(2)}, u32[]{:S(2)}) collective-permute-start(bf16[512,128]{1,0:T(8,128)(2,1)S(1)} %collective-permute-done.7.refs_5_), channel_id=1, source_target_pairs={{0,4},{1,5},{2,6},{3,7},{4,8},{5,9},{6,10},{7,11},{8,12},{9,13},{1... | collective-permute-start | bytes 393224 | tf_op jit(solution)/shard_map/ppermute | solution.py:26
  79.5 12.5 %collective-permute-start.12 = (bf16[512,128]{1,0:T(8,128)(2,1)S(1)}, bf16[512,128]{1,0:T(8,128)(2,1)S(1)}, u32[]{:S(2)}, u32[]{:S(2)}) collective-permute-start(bf16[512,128]{1,0:T(8,128)(2,1)S(1)} %collective-permute-done.11.refs_6_), channel_id=1, source_target_pairs={{0,44},{1,45},{2,46},{3,47},{4,0},{5,1},{6,2},{7,3},{8,4},{9,5},{1... | collective-permute-start | bytes 393224 | tf_op jit(solution)/shard_map/ppermute | solution.py:26
  87.1 10.1 %collective-permute-start.13 = (bf16[512,128]{1,0:T(8,128)(2,1)S(1)}, bf16[512,128]{1,0:T(8,128)(2,1)S(1)}, u32[]{:S(2)}, u32[]{:S(2)}) collective-permute-start(bf16[512,128]{1,0:T(8,128)(2,1)S(1)} %collective-permute-done.8.refs_0_), channel_id=1, source_target_pairs={{0,4},{1,5},{2,6},{3,7},{4,8},{5,9},{6,10},{7,11},{8,12},{9,13},{1... | collective-permute-start | bytes 393224 | tf_op jit(solution)/shard_map/ppermute | solution.py:26
  90.0 9.1 %collective-permute-start.1 = (bf16[128,512]{1,0:T(8,128)(2,1)S(1)}, bf16[128,512]{1,0:T(8,128)(2,1)S(1)}, u32[]{:S(2)}, u32[]{:S(2)}) collective-permute-start(bf16[128,512]{1,0:T(8,128)(2,1)S(1)} %hidden.1.own_ref), channel_id=1, source_target_pairs={{0,1},{1,0},{2,3},{3,2},{4,5},{5,4},{6,7},{7,6},{8,9},{9,8},{10,11... | collective-permute-start | bytes 393224 | tf_op jit(solution)/shard_map/ppermute | solution.py:26
  92.1 8.5 %collective-permute-start.14 = (bf16[512,128]{1,0:T(8,128)(2,1)S(1)}, bf16[512,128]{1,0:T(8,128)(2,1)S(1)}, u32[]{:S(2)}, u32[]{:S(2)}) collective-permute-start(bf16[512,128]{1,0:T(8,128)(2,1)S(1)} %collective-permute-done.12.refs_1_), channel_id=1, source_target_pairs={{0,44},{1,45},{2,46},{3,47},{4,0},{5,1},{6,2},{7,3},{8,4},{9,5},{1... | collective-permute-start | bytes 393224 | tf_op jit(solution)/shard_map/ppermute | solution.py:26
  97.2 8.1 %collective-permute-start.15 = (bf16[512,128]{1,0:T(8,128)(2,1)S(1)}, bf16[512,128]{1,0:T(8,128)(2,1)S(1)}, u32[]{:S(2)}, u32[]{:S(2)}) collective-permute-start(bf16[512,128]{1,0:T(8,128)(2,1)S(1)} %collective-permute-done.13.refs_2_), channel_id=1, source_target_pairs={{0,4},{1,5},{2,6},{3,7},{4,8},{5,9},{6,10},{7,11},{8,12},{9,13},{1... | collective-permute-start | bytes 393224 | tf_op jit(solution)/shard_map/ppermute | solution.py:26
  106.5 1.4 %copy-start.1 = (bf16[6144,128]{1,0:T(8,128)(2,1)S(1)}, bf16[6144,128]{1,0:T(8,128)(2,1)}, u32[]{:S(2)}) copy-start(bf16[6144,128]{1,0:T(8,128)(2,1)} %all-gather.3.cloned.1.call-done) | copy-start | bytes 4718596
  109.9 17.9 %collective-permute-start.17 = (bf16[12,128,128]{2,1,0:T(8,128)(2,1)S(1)}, bf16[12,128,128]{2,1,0:T(8,128)(2,1)S(1)}, u32[]{:S(2)}, u32[]{:S(2)}) collective-permute-start(bf16[12,128,128]{2,1,0:T(8,128)(2,1)S(1)} %get-tuple-element.30), channel_id=1, source_target_pairs={{0,1},{1,0},{2,3},{3,2},{4,5},{5,4},{6,7},{7,6},{8,9},{9,8},{10,11... | collective-permute-start | bytes 1179656 | tf_op jit(solution)/shard_map/ppermute | solution.py:26
  113.7 14.1 %collective-permute-start.18 = (bf16[7,128,128]{2,1,0:T(8,128)(2,1)S(1)}, bf16[7,128,128]{2,1,0:T(8,128)(2,1)S(1)}, u32[]{:S(2)}, u32[]{:S(2)}) collective-permute-start(bf16[7,128,128]{2,1,0:T(8,128)(2,1)S(1)} %get-tuple-element.32), channel_id=1, source_target_pairs={{0,1},{1,0},{2,3},{3,2},{4,5},{5,4},{6,7},{7,6},{8,9},{9,8},{10,11... | collective-permute-start | bytes 688136 | tf_op jit(solution)/shard_map/ppermute | solution.py:26
  115.7 12.1 %collective-permute-start.19 = (bf16[5,128,128]{2,1,0:T(8,128)(2,1)S(1)}, bf16[5,128,128]{2,1,0:T(8,128)(2,1)S(1)}, u32[]{:S(2)}, u32[]{:S(2)}) collective-permute-start(bf16[5,128,128]{2,1,0:T(8,128)(2,1)S(1)} %get-tuple-element.34), channel_id=1, source_target_pairs={{0,1},{1,0},{2,3},{3,2},{4,5},{5,4},{6,7},{7,6},{8,9},{9,8},{10,11... | collective-permute-start | bytes 491528 | tf_op jit(solution)/shard_map/ppermute | solution.py:26
  119.6 6.9 %collective-permute-start.16 = (f32[256,128]{1,0:T(8,128)S(1)}, f32[256,128]{1,0:T(8,128)S(1)}, u32[]{:S(2)}, u32[]{:S(2)}) collective-permute-start(f32[256,128]{1,0:T(8,128)S(1)} %get-tuple-element.26), channel_id=1, source_target_pairs={{0,1},{1,0},{2,3},{3,2},{4,5},{5,4},{6,7},{7,6},{8,9},{9,8},{10,11... | collective-permute-start | bytes 393224 | tf_op jit(solution)/shard_map/ppermute | solution.py:26
Sparse Core Ops, SparseCore 0:
  19.9 69.6 all-gather.2

commit v2 on v1

v2 whole, which is shorter than its diff:
```python
import functools

import jax
import jax.numpy as jnp
from jax import lax
from jax.experimental import pallas as pl
from jax.experimental.pallas import tpu as pltpu
from jax.sharding import PartitionSpec as P

TAPS = 3
SECTIONS = 16
NZ = 12
NY = 4
SEQ = 256
LANES = 128
VMEM_LIMIT = 48 * 1024 * 1024

PAIR = 2 * LANES
BATCHES = ((0, -1, 1, -2, 2, -3, 3), (-4, 4, -5, 5), (-6,))


def along(block, move):
    route = []
    for i in range(NZ * NY):
        z, y = move(i // NY, i % NY)
        route.append((i, (z % NZ) * NY + y))
    return lax.ppermute(block, "fsdp", route)


def from_next_section(block, flip):
    total = NZ * NY
    route = []
    for s in range(SECTIONS):
        for i in range(total):
            source = ((s + 1) % SECTIONS) * total + (i ^ flip)
            route.append((source, s * total + i))
    return lax.ppermute(block, ("section", "fsdp"), route)


def delayed(values, offset):
    rows = lax.broadcasted_iota(jnp.int32, values.shape, 0)
    return jnp.where(rows >= offset, pltpu.roll(values, offset, 0), 0.0)


def advanced(values, offset):
    length = values.shape[0]
    rows = lax.broadcasted_iota(jnp.int32, values.shape, 0)
    shifted = pltpu.roll(values, lax.rem(length - offset, length), 0)
    return jnp.where(rows < length - offset, shifted, 0.0)


def hidden_kernel(spacing_ref, saved_ref, taps_ref, out_ref):
    spacing = spacing_ref[0]
    for slot, batch in ((0, 1), (1, 0)):
        values = saved_ref[batch].astype(jnp.float32)
        conv = taps_ref[0:1, :] * values
        for tap in range(1, TAPS):
            conv = conv + taps_ref[tap : tap + 1, :] * delayed(values, tap * spacing)
        out_ref[:, slot * SEQ : (slot + 1) * SEQ] = conv.T.astype(jnp.bfloat16)


def hidden_rows(saved, taps, spacing):
    return pl.pallas_call(
        hidden_kernel,
        out_shape=jax.ShapeDtypeStruct((LANES, 2 * SEQ), jnp.bfloat16),
        in_specs=[
            pl.BlockSpec(memory_space=pltpu.SMEM),
            pl.BlockSpec(memory_space=pltpu.VMEM),
            pl.BlockSpec(memory_space=pltpu.VMEM),
        ],
        out_specs=pl.BlockSpec(memory_space=pltpu.VMEM),
        compiler_params=pltpu.CompilerParams(vmem_limit_bytes=VMEM_LIMIT),
        name="hidden",
    )(spacing, saved, taps)


def pack_kernel(*refs):
    for i in range(4):
        row, column = (i // 2) * SEQ, (i % 2) * LANES
        refs[4][row : row + SEQ, column : column + LANES] = refs[i][...]


def pack(earlier, earlier_other, received, received_other):
    whole = pl.BlockSpec(memory_space=pltpu.VMEM)
    return pl.pallas_call(
        pack_kernel,
        out_shape=jax.ShapeDtypeStruct((2 * SEQ, PAIR), jnp.bfloat16),
        in_specs=[whole] * 4,
        out_specs=whole,
        compiler_params=pltpu.CompilerParams(vmem_limit_bytes=VMEM_LIMIT),
        name="pack",
    )(earlier, earlier_other, received, received_other)


def columns_of(z, y):
    return pl.ds(pl.multiple_of((z * NY + y) * LANES, LANES), LANES)


def split_kernel(place_ref, weight_ref, keep_ref, send_ref):
    y = place_ref[1]
    for z in range(weight_ref.shape[1] // (NY * LANES)):
        for flip, lanes in ((0, slice(0, LANES)), (2, slice(LANES, PAIR))):
            keep_ref[z, :, lanes] = weight_ref[:, columns_of(z, y ^ flip)]
            send_ref[z, :, lanes] = weight_ref[:, columns_of(z, y ^ (flip + 1))]


def split_weight(place, weight):
    steps, per = 3, NZ // 3
    out = jax.ShapeDtypeStruct((NZ, LANES, PAIR), jnp.bfloat16)
    block = pl.BlockSpec((per, LANES, PAIR), lambda i: (i, 0, 0))
    return pl.pallas_call(
        split_kernel,
        out_shape=(out, out),
        grid=(steps,),
        in_specs=[
            pl.BlockSpec(memory_space=pltpu.SMEM),
            pl.BlockSpec((LANES, per * NY * LANES), lambda i: (0, i)),
        ],
        out_specs=(block, block),
        compiler_params=pltpu.CompilerParams(vmem_limit_bytes=VMEM_LIMIT),
        name="split_weight",
    )(place, weight)


def products_kernel(places, place_ref, own_ref, partner_ref, keep_ref, got_ref, *refs):
    blocks, refs = refs[: len(places)], refs[len(places) :]
    had_refs, (mine_ref, theirs_ref, back_mine_ref, back_theirs_ref) = refs[:-4], refs[-4:]
    left = jnp.concatenate([own_ref[...], partner_ref[...]], axis=0)
    if had_refs:
        back = jnp.concatenate([had_refs[0][...], had_refs[1][...]], axis=1)
    else:
        back = jnp.zeros((SEQ, PAIR), jnp.float32)
    for i, place in enumerate(places):
        block = blocks[i][...]
        grad = jnp.dot(left, block, preferred_element_type=jnp.float32)
        mine_ref[i] = grad[:LANES].astype(jnp.bfloat16)
        theirs_ref[i] = grad[LANES:].astype(jnp.bfloat16)
        at = lax.rem(place_ref[0] + (place + NZ), NZ)
        weight = jnp.concatenate([keep_ref[at], got_ref[at]], axis=0)
        back = back + lax.dot_general(
            block[SEQ:], weight, (((1,), (1,)), ((), ())), preferred_element_type=jnp.float32
        )
    back_mine_ref[...] = back[:, :LANES]
    back_theirs_ref[...] = back[:, LANES:]


def products(places, operands):
    count = len(places)
    grads = jax.ShapeDtypeStruct((count, LANES, PAIR), jnp.bfloat16)
    backs = jax.ShapeDtypeStruct((SEQ, LANES), jnp.float32)
    flops = 4 * count * PAIR * 2 * SEQ * PAIR
    whole = pl.BlockSpec(memory_space=pltpu.VMEM)
    return pl.pallas_call(
        functools.partial(products_kernel, places),
        out_shape=(grads, grads, backs, backs),
        in_specs=[pl.BlockSpec(memory_space=pltpu.SMEM)] + [whole] * (len(operands) - 1),
        out_specs=(whole,) * 4,
        compiler_params=pltpu.CompilerParams(vmem_limit_bytes=VMEM_LIMIT),
        cost_estimate=pl.CostEstimate(flops=flops, bytes_accessed=1 << 20, transcendentals=0),
        name="products",
    )(*operands)


def adjoint_kernel(spacing_ref, received_ref, saved_ref, taps_ref, mine_ref, theirs_ref, input_ref, taps_out_ref):
    spacing = spacing_ref[0]
    back = mine_ref[...] + theirs_ref[...]
    values = saved_ref[0].astype(jnp.float32)
    total = received_ref[...].astype(jnp.float32)
    for tap in range(TAPS):
        offset = tap * spacing
        total = total + taps_ref[tap : tap + 1, :] * advanced(back, offset)
        taps_out_ref[tap : tap + 1, :] = jnp.sum(back * delayed(values, offset), axis=0, keepdims=True)
    input_ref[...] = total.astype(jnp.bfloat16)


def adjoint(spacing, received, saved, taps, mine, theirs):
    whole = pl.BlockSpec(memory_space=pltpu.VMEM)
    return pl.pallas_call(
        adjoint_kernel,
        out_shape=(
            jax.ShapeDtypeStruct((SEQ, LANES), jnp.bfloat16),
            jax.ShapeDtypeStruct((TAPS, LANES), jnp.float32),
        ),
        in_specs=[pl.BlockSpec(memory_space=pltpu.SMEM)] + [whole] * 5,
        out_specs=(whole, whole),
        compiler_params=pltpu.CompilerParams(vmem_limit_bytes=VMEM_LIMIT),
        name="adjoint",
    )(spacing, received, saved, taps, mine, theirs)


def put(out_ref, z, y, source, flip):
    out_ref[:, columns_of(z, y ^ flip)] = source[:, :LANES]
    out_ref[:, columns_of(z, y ^ (flip + 2))] = source[:, LANES:]


def assemble_kernel(batches, place_ref, *refs):
    out_ref = refs[-1]
    for number, places in enumerate(batches):
        for i, place in enumerate(places):
            at = lax.rem(place_ref[0] + (place + NZ), NZ)
            put(out_ref, at, place_ref[1], refs[2 * number][i], 0)
            put(out_ref, at, place_ref[1], refs[2 * number + 1][i], 1)


def assemble(place, batches, pieces):
    whole = pl.BlockSpec(memory_space=pltpu.VMEM)
    return pl.pallas_call(
        functools.partial(assemble_kernel, batches),
        out_shape=jax.ShapeDtypeStruct((LANES, NZ * NY * LANES), jnp.bfloat16),
        in_specs=[pl.BlockSpec(memory_space=pltpu.SMEM)] + [whole] * len(pieces),
        out_specs=whole,
        compiler_params=pltpu.CompilerParams(vmem_limit_bytes=VMEM_LIMIT),
        name="assemble",
    )(place, *pieces)


def finish_kernel(place_ref, mine_ref, got_ref, whole_ref, out_ref):
    put(out_ref, 0, place_ref[1], mine_ref[0], 0)
    put(out_ref, 0, place_ref[1], got_ref[0], 1)


def finish(place, mine, got, whole):
    piece = pl.BlockSpec((1, LANES, PAIR), lambda i, place: (0, 0, 0))
    return pl.pallas_call(
        finish_kernel,
        out_shape=jax.ShapeDtypeStruct(whole.shape, whole.dtype),
        grid_spec=pltpu.PrefetchScalarGridSpec(
            num_scalar_prefetch=1,
            grid=(1,),
            in_specs=[piece, piece, pl.BlockSpec(memory_space=pl.ANY)],
            out_specs=pl.BlockSpec((LANES, NY * LANES), lambda i, place: (0, lax.rem(place[0] + NZ // 2, NZ))),
        ),
        input_output_aliases={3: 0},
        name="finish",
    )(place, mine, got, whole)


def per_device(saved_input, incoming, earlier_grad, w_out, kernel, dilation):
    saved, taps, weight = saved_input[0], kernel[0], w_out[0]
    earlier = earlier_grad[0]
    index = lax.axis_index("fsdp")
    place = jnp.stack([lax.div(index, NY), lax.rem(index, NY)]).astype(jnp.int32)
    partner = lambda z, y: (z, y ^ 1)

    received = from_next_section(incoming[0], 0)
    received_other = from_next_section(incoming[0], 2)
    earlier_other = along(earlier, lambda z, y: (z, y ^ 2))
    ring = {0: pack(earlier, earlier_other, received, received_other)}
    for step in range(1, NZ // 2 + 1):
        ring[-step] = along(ring[1 - step], lambda z, y: (z + 1, y))
        if step < NZ // 2:
            ring[step] = along(ring[step - 1], lambda z, y: (z - 1, y))

    rows = hidden_rows(saved, taps, dilation)
    rows_partner = along(rows, partner)
    keep, send = split_weight(place, weight)
    got = along(send, partner)

    backs, pieces = (), []
    for places in BATCHES:
        mine, theirs, *backs = products(places, (place, rows, rows_partner, keep, got, *(ring[p] for p in places), *backs))
        if places == BATCHES[-1]:
            back_other = along(backs[1], partner)
        pieces += [mine, along(theirs, partner)]
    grad_input, grad_kernel = adjoint(dilation, received, saved, taps, backs[0], back_other)
    grad_weight = finish(place, *pieces[-2:], assemble(place, BATCHES[:-1], pieces[:-2]))
    return grad_input[None], grad_kernel[None], grad_weight[None]


def solution(mesh):
    return jax.shard_map(
        per_device,
        mesh=mesh,
        in_specs=(
            P("section", None, None, "fsdp"),
            P("section", None, "fsdp"),
            P("section", None, "fsdp"),
            P("section", "fsdp", None),
            P("section", None, "fsdp"),
            P("section"),
        ),
        out_specs=(
            P("section", None, "fsdp"),
            P("section", None, "fsdp"),
            P("section", "fsdp", None),
        ),
        check_vma=False,
    )
```

time: 138 us -> 109 us (0.79)
  the two profiles are of different devices: /device:TPU:8 before, /device:TPU:6 now
where the time goes in v2:
time: 109 us; the launch traced here: 107 us
  starting transfers between devices  73.1 us (67%)
  waiting for transfers between devices  19.4 us (18%)
  Pallas kernels  9.85 us (9%)
  local copies, waits for them, and re-layouts  3.45 us (3%)
  between operations  1.62 us (1%)
    ppermute x18, starting transfers between devices, along(): return lax.ppermute(block, 'fsdp', route)  68.7 us
    ppermute x18, waiting for transfers between devices, along(): return lax.ppermute(block, 'fsdp', route)  16.5 us
    ppermute x2, starting transfers between devices, from_next_section(): return lax.ppermute(block, ('section', 'fsdp'), route)  4.38 us
    unnamed x16, local copies, waits for them, and re-layouts  3.45 us
    pallas_call x3, Pallas kernels, products(): pl.pallas_call(functools.partial(products_kernel, places), out_shape=(gra...  3.39 us
    ppermute x2, waiting for transfers between devices, from_next_section(): return lax.ppermute(block, ('section', 'fsdp'), route)  2.92 us
    pallas_call x1, Pallas kernels, finish(): pl.pallas_call(finish_kernel, out_shape=jax.ShapeDtypeStruct(whole.shape,...  2.21 us
  transfers between devices with their start and end apart: 20, of which 9 were waited for; matrix products, arithmetic and copies ran while one was open for 0% of the time, Pallas kernels for 8%

profile of v2, /device:TPU:6, one launch (start us, length us, event | category | flops | bytes accessed | tf_op | source)
XLA Modules:
  0.0 107.5 jit_solution(225932348564055332)
XLA Ops:
  0.6 2.3 %collective-permute-start = (bf16[256,128]{1,0:T(8,128)(2,1)}, bf16[256,128]{1,0:T(8,128)(2,1)S(1)}, u32[]{:S(2)}, u32[]{:S(2)}) collective-permute-start(bf16[256,128]{1,0:T(8,128)(2,1)} %bitcast.21), channel_id=1, source_target_pairs={{48,0},{49,1},{50,2},{51,3},{52,4},{53,5},{54,6},{55,7},{56,8},{57... | collective-permute-start | bytes 196616 | tf_op jit(solution)/shard_map/ppermute | solution.py:37
  3.0 4.5 %collective-permute-start.3 = (bf16[256,128]{1,0:T(8,128)(2,1)}, bf16[256,128]{1,0:T(8,128)(2,1)S(1)}, u32[]{:S(2)}, u32[]{:S(2)}) collective-permute-start(bf16[256,128]{1,0:T(8,128)(2,1)} %bitcast.15), channel_id=1, source_target_pairs={{0,2},{1,3},{2,0},{3,1},{4,6},{5,7},{6,4},{7,5},{8,10},{9,11},{10,... | collective-permute-start | bytes 196616 | tf_op jit(solution)/shard_map/ppermute | solution.py:27
  7.5 2.1 %collective-permute-start.4 = (bf16[256,128]{1,0:T(8,128)(2,1)}, bf16[256,128]{1,0:T(8,128)(2,1)S(1)}, u32[]{:S(2)}, u32[]{:S(2)}) collective-permute-start(bf16[256,128]{1,0:T(8,128)(2,1)} %bitcast.22), channel_id=1, source_target_pairs={{50,0},{51,1},{48,2},{49,3},{54,4},{55,5},{52,6},{53,7},{58,8},{59... | collective-permute-start | bytes 196616 | tf_op jit(solution)/shard_map/ppermute | solution.py:37
  9.6 2.1 %collective-permute-done.3.refs_1_ = bf16[256,128]{1,0:T(8,128)(2,1)S(1)} collective-permute-done((bf16[256,128]{1,0:T(8,128)(2,1)}, bf16[256,128]{1,0:T(8,128)(2,1)S(1)}, u32[]{:S(2)}, u32[]{:S(2)}) %collective-permute-start.3) | collective-permute-done | bytes 65568 | tf_op jit(solution)/shard_map/ppermute | solution.py:27
  11.6 2.9 %collective-permute-done.4.refs_3_ = bf16[256,128]{1,0:T(8,128)(2,1)S(1)} collective-permute-done((bf16[256,128]{1,0:T(8,128)(2,1)}, bf16[256,128]{1,0:T(8,128)(2,1)S(1)}, u32[]{:S(2)}, u32[]{:S(2)}) %collective-permute-start.4) | collective-permute-done | bytes 65568 | tf_op jit(solution)/shard_map/ppermute | solution.py:37
  14.5 0.8 copy-done.3
  15.4 4.3 %collective-permute-start.5 = (bf16[512,256]{1,0:T(8,128)(2,1)S(1)}, bf16[512,256]{1,0:T(8,128)(2,1)S(1)}, u32[]{:S(2)}, u32[]{:S(2)}) collective-permute-start(bf16[512,256]{1,0:T(8,128)(2,1)S(1)} %pack.1.refs_0_), channel_id=1, source_target_pairs={{0,4},{1,5},{2,6},{3,7},{4,8},{5,9},{6,10},{7,11},{8,12},{9,13},{1... | collective-permute-start | bytes 786440 | tf_op jit(solution)/shard_map/ppermute | solution.py:27
  19.7 12.2 %collective-permute-start.11 = (bf16[512,256]{1,0:T(8,128)(2,1)S(1)}, bf16[512,256]{1,0:T(8,128)(2,1)S(1)}, u32[]{:S(2)}, u32[]{:S(2)}) collective-permute-start(bf16[512,256]{1,0:T(8,128)(2,1)S(1)} %pack.1.refs_0_), channel_id=1, source_target_pairs={{0,44},{1,45},{2,46},{3,47},{4,0},{5,1},{6,2},{7,3},{8,4},{9,5},{1... | collective-permute-start | bytes 786440 | tf_op jit(solution)/shard_map/ppermute | solution.py:27
  32.0 2.4 %collective-permute-done.5.refs_1_ = bf16[512,256]{1,0:T(8,128)(2,1)S(1)} collective-permute-done((bf16[512,256]{1,0:T(8,128)(2,1)S(1)}, bf16[512,256]{1,0:T(8,128)(2,1)S(1)}, u32[]{:S(2)}, u32[]{:S(2)}) %collective-permute-start.5) | collective-permute-done | bytes 262176 | tf_op jit(solution)/shard_map/ppermute | solution.py:27
  34.4 1.9 %collective-permute-start.6 = (bf16[512,256]{1,0:T(8,128)(2,1)S(1)}, bf16[512,256]{1,0:T(8,128)(2,1)S(1)}, u32[]{:S(2)}, u32[]{:S(2)}) collective-permute-start(bf16[512,256]{1,0:T(8,128)(2,1)S(1)} %collective-permute-done.5.refs_1_), channel_id=1, source_target_pairs={{0,4},{1,5},{2,6},{3,7},{4,8},{5,9},{6,10},{7,11},{8,12},{9,13},{1... | collective-permute-start | bytes 786440 | tf_op jit(solution)/shard_map/ppermute | solution.py:27
  36.3 0.0 collective-permute-done.11.refs_2_
  36.3 5.3 %collective-permute-start.12 = (bf16[512,256]{1,0:T(8,128)(2,1)S(1)}, bf16[512,256]{1,0:T(8,128)(2,1)S(1)}, u32[]{:S(2)}, u32[]{:S(2)}) collective-permute-start(bf16[512,256]{1,0:T(8,128)(2,1)S(1)} %collective-permute-done.11.refs_2_), channel_id=1, source_target_pairs={{0,44},{1,45},{2,46},{3,47},{4,0},{5,1},{6,2},{7,3},{8,4},{9,5},{1... | collective-permute-start | bytes 786440 | tf_op jit(solution)/shard_map/ppermute | solution.py:27
  41.6 0.1 pad_add_fusion.place_ref
  41.7 1.4 %copy-done = bf16[1,128,6144]{2,1,0:T(8,128)(2,1)S(1)} copy-done((bf16[1,128,6144]{2,1,0:T(8,128)(2,1)S(1)}, bf16[1,128,6144]{2,1,0:T(8,128)(2,1)}, u32[]{:S(2)}) %copy-start) | copy-done | bytes 1572888
  43.1 1.1 %split_weight.1 = (bf16[12,128,256]{2,1,0:T(8,128)(2,1)S(1)}, bf16[12,128,256]{2,1,0:T(8,128)(2,1)S(1)}) custom-call(s32[2]{0:T(128)S(1)} %pad_add_fusion.place_ref, bf16[128,6144]{1,0:T(8,128)(2,1)S(1)} %bitcast.12), custom_call_target="tpu_custom_call" | custom-call | tf_op jit(solution)/shard_map/split_weight/pallas_call | solution.py:111
  44.2 3.7 %collective-permute-start.2 = (bf16[12,128,256]{2,1,0:T(8,128)(2,1)S(1)}, bf16[12,128,256]{2,1,0:T(8,128)(2,1)S(1)}, u32[]{:S(2)}, u32[]{:S(2)}) collective-permute-start(bf16[12,128,256]{2,1,0:T(8,128)(2,1)S(1)} %get-tuple-element.20), channel_id=1, source_target_pairs={{0,1},{1,0},{2,3},{3,2},{4,5},{5,4},{6,7},{7,6},{8,9},{9,8},{10,11... | collective-permute-start | bytes 2359304 | tf_op jit(solution)/shard_map/ppermute | solution.py:27
  47.9 0.0 collective-permute-done.6.refs_3_
  47.9 1.9 %collective-permute-start.7 = (bf16[512,256]{1,0:T(8,128)(2,1)S(1)}, bf16[512,256]{1,0:T(8,128)(2,1)S(1)}, u32[]{:S(2)}, u32[]{:S(2)}) collective-permute-start(bf16[512,256]{1,0:T(8,128)(2,1)S(1)} %collective-permute-done.6.refs_3_), channel_id=1, source_target_pairs={{0,4},{1,5},{2,6},{3,7},{4,8},{5,9},{6,10},{7,11},{8,12},{9,13},{1... | collective-permute-start | bytes 786440 | tf_op jit(solution)/shard_map/ppermute | solution.py:27
  49.9 0.0 collective-permute-done.12.refs_4_
  49.9 5.1 %collective-permute-start.13 = (bf16[512,256]{1,0:T(8,128)(2,1)S(1)}, bf16[512,256]{1,0:T(8,128)(2,1)S(1)}, u32[]{:S(2)}, u32[]{:S(2)}) collective-permute-start(bf16[512,256]{1,0:T(8,128)(2,1)S(1)} %collective-permute-done.12.refs_4_), channel_id=1, source_target_pairs={{0,44},{1,45},{2,46},{3,47},{4,0},{5,1},{6,2},{7,3},{8,4},{9,5},{1... | collective-permute-start | bytes 786440 | tf_op jit(solution)/shard_map/ppermute | solution.py:27
  55.0 4.4 %collective-permute-done.7.refs_5_ = bf16[512,256]{1,0:T(8,128)(2,1)S(1)} collective-permute-done((bf16[512,256]{1,0:T(8,128)(2,1)S(1)}, bf16[512,256]{1,0:T(8,128)(2,1)S(1)}, u32[]{:S(2)}, u32[]{:S(2)}) %collective-permute-start.7) | collective-permute-done | bytes 262176 | tf_op jit(solution)/shard_map/ppermute | solution.py:27
  59.5 1.9 %collective-permute-start.8 = (bf16[512,256]{1,0:T(8,128)(2,1)S(1)}, bf16[512,256]{1,0:T(8,128)(2,1)S(1)}, u32[]{:S(2)}, u32[]{:S(2)}) collective-permute-start(bf16[512,256]{1,0:T(8,128)(2,1)S(1)} %collective-permute-done.7.refs_5_), channel_id=1, source_target_pairs={{0,4},{1,5},{2,6},{3,7},{4,8},{5,9},{6,10},{7,11},{8,12},{9,13},{1... | collective-permute-start | bytes 786440 | tf_op jit(solution)/shard_map/ppermute | solution.py:27
  61.4 0.0 collective-permute-done.13.refs_6_
  61.4 5.5 %collective-permute-start.14 = (bf16[512,256]{1,0:T(8,128)(2,1)S(1)}, bf16[512,256]{1,0:T(8,128)(2,1)S(1)}, u32[]{:S(2)}, u32[]{:S(2)}) collective-permute-start(bf16[512,256]{1,0:T(8,128)(2,1)S(1)} %collective-permute-done.13.refs_6_), channel_id=1, source_target_pairs={{0,44},{1,45},{2,46},{3,47},{4,0},{5,1},{6,2},{7,3},{8,4},{9,5},{1... | collective-permute-start | bytes 786440 | tf_op jit(solution)/shard_map/ppermute | solution.py:27
  67.5 0.3 hidden.1.own_ref
  67.8 1.9 %collective-permute-start.1 = (bf16[128,512]{1,0:T(8,128)(2,1)S(1)}, bf16[128,512]{1,0:T(8,128)(2,1)S(1)}, u32[]{:S(2)}, u32[]{:S(2)}) collective-permute-start(bf16[128,512]{1,0:T(8,128)(2,1)S(1)} %hidden.1.own_ref), channel_id=1, source_target_pairs={{0,1},{1,0},{2,3},{3,2},{4,5},{5,4},{6,7},{7,6},{8,9},{9,8},{10,11... | collective-permute-start | bytes 393224 | tf_op jit(solution)/shard_map/ppermute | solution.py:27
  69.8 1.6 %collective-permute-done.8.refs_0_ = bf16[512,256]{1,0:T(8,128)(2,1)S(1)} collective-permute-done((bf16[512,256]{1,0:T(8,128)(2,1)S(1)}, bf16[512,256]{1,0:T(8,128)(2,1)S(1)}, u32[]{:S(2)}, u32[]{:S(2)}) %collective-permute-start.8) | collective-permute-done | bytes 262176 | tf_op jit(solution)/shard_map/ppermute | solution.py:27
  71.3 1.9 %collective-permute-start.9 = (bf16[512,256]{1,0:T(8,128)(2,1)S(1)}, bf16[512,256]{1,0:T(8,128)(2,1)S(1)}, u32[]{:S(2)}, u32[]{:S(2)}) collective-permute-start(bf16[512,256]{1,0:T(8,128)(2,1)S(1)} %collective-permute-done.8.refs_0_), channel_id=1, source_target_pairs={{0,4},{1,5},{2,6},{3,7},{4,8},{5,9},{6,10},{7,11},{8,12},{9,13},{1... | collective-permute-start | bytes 786440 | tf_op jit(solution)/shard_map/ppermute | solution.py:27
  73.3 5.1 %collective-permute-start.15 = (bf16[512,256]{1,0:T(8,128)(2,1)S(1)}, bf16[512,256]{1,0:T(8,128)(2,1)S(1)}, u32[]{:S(2)}, u32[]{:S(2)}) collective-permute-start(bf16[512,256]{1,0:T(8,128)(2,1)S(1)} %collective-permute-done.14.refs_1_), channel_id=1, source_target_pairs={{0,44},{1,45},{2,46},{3,47},{4,0},{5,1},{6,2},{7,3},{8,4},{9,5},{1... | collective-permute-start | bytes 786440 | tf_op jit(solution)/shard_map/ppermute | solution.py:27
  78.4 0.0 collective-permute-done.1.partner_ref
  78.4 1.4 %products.3 = (bf16[7,128,256]{2,1,0:T(8,128)(2,1)S(1)}, bf16[7,128,256]{2,1,0:T(8,128)(2,1)S(1)}, f32[256,128]{1,0:T(8,128)S(1)}, f32[256,128]{1,0:T(8,128)S(1)}) custom-call(s32[2]{0:T(128)S(1)} %pad_add_fusion.place_ref, bf16[128,512]{1,0:T(8,128)(2,1)S(1)} %hidden.1.own_ref, bf16[128,512]{1,0:T(8,128)(2,1)S(1)} %collective-permute-done.1.partner_ref, ...), custom_call_target="tpu_custom_call" | custom-call | flops 939524096 | bytes 1048576 | tf_op jit(solution)/shard_map/products/pallas_call | solution.py:153
  79.9 2.4 %collective-permute-start.18 = (bf16[7,128,256]{2,1,0:T(8,128)(2,1)S(1)}, bf16[7,128,256]{2,1,0:T(8,128)(2,1)S(1)}, u32[]{:S(2)}, u32[]{:S(2)}) collective-permute-start(bf16[7,128,256]{2,1,0:T(8,128)(2,1)S(1)} %get-tuple-element.32), channel_id=1, source_target_pairs={{0,1},{1,0},{2,3},{3,2},{4,5},{5,4},{6,7},{7,6},{8,9},{9,8},{10,11... | collective-permute-start | bytes 1376264 | tf_op jit(solution)/shard_map/ppermute | solution.py:27
  82.3 0.2 collective-permute-done.9.refs_2_
  82.5 1.9 %collective-permute-start.10 = (bf16[512,256]{1,0:T(8,128)(2,1)S(1)}, bf16[512,256]{1,0:T(8,128)(2,1)S(1)}, u32[]{:S(2)}, u32[]{:S(2)}) collective-permute-start(bf16[512,256]{1,0:T(8,128)(2,1)S(1)} %collective-permute-done.9.refs_2_), channel_id=1, source_target_pairs={{0,4},{1,5},{2,6},{3,7},{4,8},{5,9},{6,10},{7,11},{8,12},{9,13},{1... | collective-permute-start | bytes 786440 | tf_op jit(solution)/shard_map/ppermute | solution.py:27
  84.4 1.1 %products.4 = (bf16[4,128,256]{2,1,0:T(8,128)(2,1)S(1)}, bf16[4,128,256]{2,1,0:T(8,128)(2,1)S(1)}, f32[256,128]{1,0:T(8,128)S(1)}, f32[256,128]{1,0:T(8,128)S(1)}) custom-call(s32[2]{0:T(128)S(1)} %pad_add_fusion.place_ref, bf16[128,512]{1,0:T(8,128)(2,1)S(1)} %hidden.1.own_ref, bf16[128,512]{1,0:T(8,128)(2,1)S(1)} %collective-permute-done.1.partner_ref, ...), custom_call_target="tpu_custom_call" | custom-call | flops 536870912 | bytes 1048576 | tf_op jit(solution)/shard_map/products/pallas_call | solution.py:153
  85.5 3.3 %collective-permute-start.19 = (bf16[4,128,256]{2,1,0:T(8,128)(2,1)S(1)}, bf16[4,128,256]{2,1,0:T(8,128)(2,1)S(1)}, u32[]{:S(2)}, u32[]{:S(2)}) collective-permute-start(bf16[4,128,256]{2,1,0:T(8,128)(2,1)S(1)} %get-tuple-element.34), channel_id=1, source_target_pairs={{0,1},{1,0},{2,3},{3,2},{4,5},{5,4},{6,7},{7,6},{8,9},{9,8},{10,11... | collective-permute-start | bytes 786440 | tf_op jit(solution)/shard_map/ppermute | solution.py:27
  88.8 3.9 %collective-permute-done.10.refs_0_ = bf16[512,256]{1,0:T(8,128)(2,1)S(1)} collective-permute-done((bf16[512,256]{1,0:T(8,128)(2,1)S(1)}, bf16[512,256]{1,0:T(8,128)(2,1)S(1)}, u32[]{:S(2)}, u32[]{:S(2)}) %collective-permute-start.10) | collective-permute-done | bytes 262176 | tf_op jit(solution)/shard_map/ppermute | solution.py:27
  92.7 0.8 products.5
  93.5 0.0 copy-start.2
  93.5 3.3 %collective-permute-start.16 = (f32[256,128]{1,0:T(8,128)S(1)}, f32[256,128]{1,0:T(8,128)S(1)}, u32[]{:S(2)}, u32[]{:S(2)}) collective-permute-start(f32[256,128]{1,0:T(8,128)S(1)} %get-tuple-element.26), channel_id=1, source_target_pairs={{0,1},{1,0},{2,3},{3,2},{4,5},{5,4},{6,7},{7,6},{8,9},{9,8},{10,11... | collective-permute-start | bytes 393224 | tf_op jit(solution)/shard_map/ppermute | solution.py:27
  96.9 2.5 %collective-permute-start.17 = (bf16[1,128,256]{2,1,0:T(8,128)(2,1)S(1)}, bf16[1,128,256]{2,1,0:T(8,128)(2,1)S(1)}, u32[]{:S(2)}, u32[]{:S(2)}) collective-permute-start(bf16[1,128,256]{2,1,0:T(8,128)(2,1)S(1)} %get-tuple-element.30), channel_id=1, source_target_pairs={{0,1},{1,0},{2,3},{3,2},{4,5},{5,4},{6,7},{7,6},{8,9},{9,8},{10,11... | collective-permute-start | bytes 196616 | tf_op jit(solution)/shard_map/ppermute | solution.py:27
  99.4 1.4 %collective-permute-done.19.refs_3_ = bf16[4,128,256]{2,1,0:T(8,128)(2,1)S(1)} collective-permute-done((bf16[4,128,256]{2,1,0:T(8,128)(2,1)S(1)}, bf16[4,128,256]{2,1,0:T(8,128)(2,1)S(1)}, u32[]{:S(2)}, u32[]{:S(2)}) %collective-permute-start.19) | collective-permute-done | bytes 262176 | tf_op jit(solution)/shard_map/ppermute | solution.py:27
  100.8 2.0 %assemble.1.whole_ref = bf16[128,6144]{1,0:T(8,128)(2,1)} custom-call(s32[2]{0:T(128)S(1)} %pad_add_fusion.place_ref, bf16[7,128,256]{2,1,0:T(8,128)(2,1)S(1)} %get-tuple-element.31.refs_0_, bf16[7,128,256]{2,1,0:T(8,128)(2,1)S(1)} %collective-permute-done.18.refs_1_, bf16[4,128,256]{2,1,0:T(8,128)(2,1)S(1)} %get-tuple-element.33.refs_2_, ...), custom_call_target="tpu_custom_call" | custom-call | tf_op jit(solution)/shard_map/assemble/pallas_call | solution.py:207
  102.8 0.4 collective-permute-done.17.got_ref
  103.3 0.6 copy-done.5
  103.9 2.2 %finish.1 = bf16[128,6144]{1,0:T(8,128)(2,1)} custom-call(s32[2]{0:T(128)} %copy-done.4, bf16[1,128,256]{2,1,0:T(8,128)(2,1)} %copy-done.2, bf16[1,128,256]{2,1,0:T(8,128)(2,1)} %copy-done.5, bf16[128,6144]{1,0:T(8,128)(2,1)} %assemble.1.whole_ref), custom_call_target="tpu_custom_call", output_to_operand_aliasing={{}: (3, {})} | custom-call | tf_op jit(solution)/shard_map/finish/pallas_call | solution.py:224
  106.1 0.8 adjoint.1
  106.9 0.6 copy.10
  (18 shorter events, 0.1 us)
Async XLA Ops:
  0.6 66.9 %copy-start.1 = (bf16[1,2,256,128]{3,2,1,0:T(8,128)(2,1)S(1)}, bf16[1,2,256,128]{3,2,1,0:T(8,128)(2,1)}, u32[]{:S(2)}) copy-start(bf16[1,2,256,128]{3,2,1,0:T(8,128)(2,1)} %param.6) | copy-start | bytes 393220
  0.6 8.9 %collective-permute-start = (bf16[256,128]{1,0:T(8,128)(2,1)}, bf16[256,128]{1,0:T(8,128)(2,1)S(1)}, u32[]{:S(2)}, u32[]{:S(2)}) collective-permute-start(bf16[256,128]{1,0:T(8,128)(2,1)} %bitcast.21), channel_id=1, source_target_pairs={{48,0},{49,1},{50,2},{51,3},{52,4},{53,5},{54,6},{55,7},{56,8},{57... | collective-permute-start | bytes 196616 | tf_op jit(solution)/shard_map/ppermute | solution.py:37
  3.0 8.7 %collective-permute-start.3 = (bf16[256,128]{1,0:T(8,128)(2,1)}, bf16[256,128]{1,0:T(8,128)(2,1)S(1)}, u32[]{:S(2)}, u32[]{:S(2)}) collective-permute-start(bf16[256,128]{1,0:T(8,128)(2,1)} %bitcast.15), channel_id=1, source_target_pairs={{0,2},{1,3},{2,0},{3,1},{4,6},{5,7},{6,4},{7,5},{8,10},{9,11},{10,... | collective-permute-start | bytes 196616 | tf_op jit(solution)/shard_map/ppermute | solution.py:27
  7.5 7.1 %collective-permute-start.4 = (bf16[256,128]{1,0:T(8,128)(2,1)}, bf16[256,128]{1,0:T(8,128)(2,1)S(1)}, u32[]{:S(2)}, u32[]{:S(2)}) collective-permute-start(bf16[256,128]{1,0:T(8,128)(2,1)} %bitcast.22), channel_id=1, source_target_pairs={{50,0},{51,1},{48,2},{49,3},{54,4},{55,5},{52,6},{53,7},{58,8},{59... | collective-permute-start | bytes 196616 | tf_op jit(solution)/shard_map/ppermute | solution.py:37
  14.5 0.8 copy-start.3
  15.4 51.5 %copy-start.6 = (f32[1,3,128]{2,0,1:T(1,128)S(1)}, f32[1,3,128]{2,0,1:T(1,128)}, u32[]{:S(2)}) copy-start(f32[1,3,128]{2,0,1:T(1,128)} %param.10) | copy-start | bytes 4612
  15.4 18.9 %collective-permute-start.5 = (bf16[512,256]{1,0:T(8,128)(2,1)S(1)}, bf16[512,256]{1,0:T(8,128)(2,1)S(1)}, u32[]{:S(2)}, u32[]{:S(2)}) collective-permute-start(bf16[512,256]{1,0:T(8,128)(2,1)S(1)} %pack.1.refs_0_), channel_id=1, source_target_pairs={{0,4},{1,5},{2,6},{3,7},{4,8},{5,9},{6,10},{7,11},{8,12},{9,13},{1... | collective-permute-start | bytes 786440 | tf_op jit(solution)/shard_map/ppermute | solution.py:27
  19.7 16.6 %collective-permute-start.11 = (bf16[512,256]{1,0:T(8,128)(2,1)S(1)}, bf16[512,256]{1,0:T(8,128)(2,1)S(1)}, u32[]{:S(2)}, u32[]{:S(2)}) collective-permute-start(bf16[512,256]{1,0:T(8,128)(2,1)S(1)} %pack.1.refs_0_), channel_id=1, source_target_pairs={{0,44},{1,45},{2,46},{3,47},{4,0},{5,1},{6,2},{7,3},{8,4},{9,5},{1... | collective-permute-start | bytes 786440 | tf_op jit(solution)/shard_map/ppermute | solution.py:27
  34.4 13.6 %collective-permute-start.6 = (bf16[512,256]{1,0:T(8,128)(2,1)S(1)}, bf16[512,256]{1,0:T(8,128)(2,1)S(1)}, u32[]{:S(2)}, u32[]{:S(2)}) collective-permute-start(bf16[512,256]{1,0:T(8,128)(2,1)S(1)} %collective-permute-done.5.refs_1_), channel_id=1, source_target_pairs={{0,4},{1,5},{2,6},{3,7},{4,8},{5,9},{6,10},{7,11},{8,12},{9,13},{1... | collective-permute-start | bytes 786440 | tf_op jit(solution)/shard_map/ppermute | solution.py:27
  36.3 13.5 %collective-permute-start.12 = (bf16[512,256]{1,0:T(8,128)(2,1)S(1)}, bf16[512,256]{1,0:T(8,128)(2,1)S(1)}, u32[]{:S(2)}, u32[]{:S(2)}) collective-permute-start(bf16[512,256]{1,0:T(8,128)(2,1)S(1)} %collective-permute-done.11.refs_2_), channel_id=1, source_target_pairs={{0,44},{1,45},{2,46},{3,47},{4,0},{5,1},{6,2},{7,3},{8,4},{9,5},{1... | collective-permute-start | bytes 786440 | tf_op jit(solution)/shard_map/ppermute | solution.py:27
  41.6 59.2 %copy-start.4 = (s32[2]{0:T(128)}, s32[2]{0:T(128)S(1)}, u32[]{:S(2)}) copy-start(s32[2]{0:T(128)S(1)} %pad_add_fusion.place_ref) | copy-start | bytes 28
  41.6 1.4 %copy-start = (bf16[1,128,6144]{2,1,0:T(8,128)(2,1)S(1)}, bf16[1,128,6144]{2,1,0:T(8,128)(2,1)}, u32[]{:S(2)}) copy-start(bf16[1,128,6144]{2,1,0:T(8,128)(2,1)} %param.9) | copy-start | bytes 4718596
  44.2 34.2 %collective-permute-start.2 = (bf16[12,128,256]{2,1,0:T(8,128)(2,1)S(1)}, bf16[12,128,256]{2,1,0:T(8,128)(2,1)S(1)}, u32[]{:S(2)}, u32[]{:S(2)}) collective-permute-start(bf16[12,128,256]{2,1,0:T(8,128)(2,1)S(1)} %get-tuple-element.20), channel_id=1, source_target_pairs={{0,1},{1,0},{2,3},{3,2},{4,5},{5,4},{6,7},{7,6},{8,9},{9,8},{10,11... | collective-permute-start | bytes 2359304 | tf_op jit(solution)/shard_map/ppermute | solution.py:27
  47.9 11.5 %collective-permute-start.7 = (bf16[512,256]{1,0:T(8,128)(2,1)S(1)}, bf16[512,256]{1,0:T(8,128)(2,1)S(1)}, u32[]{:S(2)}, u32[]{:S(2)}) collective-permute-start(bf16[512,256]{1,0:T(8,128)(2,1)S(1)} %collective-permute-done.6.refs_3_), channel_id=1, source_target_pairs={{0,4},{1,5},{2,6},{3,7},{4,8},{5,9},{6,10},{7,11},{8,12},{9,13},{1... | collective-permute-start | bytes 786440 | tf_op jit(solution)/shard_map/ppermute | solution.py:27
  49.9 11.5 %collective-permute-start.13 = (bf16[512,256]{1,0:T(8,128)(2,1)S(1)}, bf16[512,256]{1,0:T(8,128)(2,1)S(1)}, u32[]{:S(2)}, u32[]{:S(2)}) collective-permute-start(bf16[512,256]{1,0:T(8,128)(2,1)S(1)} %collective-permute-done.12.refs_4_), channel_id=1, source_target_pairs={{0,44},{1,45},{2,46},{3,47},{4,0},{5,1},{6,2},{7,3},{8,4},{9,5},{1... | collective-permute-start | bytes 786440 | tf_op jit(solution)/shard_map/ppermute | solution.py:27
  59.5 11.9 %collective-permute-start.8 = (bf16[512,256]{1,0:T(8,128)(2,1)S(1)}, bf16[512,256]{1,0:T(8,128)(2,1)S(1)}, u32[]{:S(2)}, u32[]{:S(2)}) collective-permute-start(bf16[512,256]{1,0:T(8,128)(2,1)S(1)} %collective-permute-done.7.refs_5_), channel_id=1, source_target_pairs={{0,4},{1,5},{2,6},{3,7},{4,8},{5,9},{6,10},{7,11},{8,12},{9,13},{1... | collective-permute-start | bytes 786440 | tf_op jit(solution)/shard_map/ppermute | solution.py:27
  61.4 11.9 %collective-permute-start.14 = (bf16[512,256]{1,0:T(8,128)(2,1)S(1)}, bf16[512,256]{1,0:T(8,128)(2,1)S(1)}, u32[]{:S(2)}, u32[]{:S(2)}) collective-permute-start(bf16[512,256]{1,0:T(8,128)(2,1)S(1)} %collective-permute-done.13.refs_6_), channel_id=1, source_target_pairs={{0,44},{1,45},{2,46},{3,47},{4,0},{5,1},{6,2},{7,3},{8,4},{9,5},{1... | collective-permute-start | bytes 786440 | tf_op jit(solution)/shard_map/ppermute | solution.py:27
  67.8 10.6 %collective-permute-start.1 = (bf16[128,512]{1,0:T(8,128)(2,1)S(1)}, bf16[128,512]{1,0:T(8,128)(2,1)S(1)}, u32[]{:S(2)}, u32[]{:S(2)}) collective-permute-start(bf16[128,512]{1,0:T(8,128)(2,1)S(1)} %hidden.1.own_ref), channel_id=1, source_target_pairs={{0,1},{1,0},{2,3},{3,2},{4,5},{5,4},{6,7},{7,6},{8,9},{9,8},{10,11... | collective-permute-start | bytes 393224 | tf_op jit(solution)/shard_map/ppermute | solution.py:27
  71.3 11.1 %collective-permute-start.9 = (bf16[512,256]{1,0:T(8,128)(2,1)S(1)}, bf16[512,256]{1,0:T(8,128)(2,1)S(1)}, u32[]{:S(2)}, u32[]{:S(2)}) collective-permute-start(bf16[512,256]{1,0:T(8,128)(2,1)S(1)} %collective-permute-done.8.refs_0_), channel_id=1, source_target_pairs={{0,4},{1,5},{2,6},{3,7},{4,8},{5,9},{6,10},{7,11},{8,12},{9,13},{1... | collective-permute-start | bytes 786440 | tf_op jit(solution)/shard_map/ppermute | solution.py:27
  73.3 11.1 %collective-permute-start.15 = (bf16[512,256]{1,0:T(8,128)(2,1)S(1)}, bf16[512,256]{1,0:T(8,128)(2,1)S(1)}, u32[]{:S(2)}, u32[]{:S(2)}) collective-permute-start(bf16[512,256]{1,0:T(8,128)(2,1)S(1)} %collective-permute-done.14.refs_1_), channel_id=1, source_target_pairs={{0,44},{1,45},{2,46},{3,47},{4,0},{5,1},{6,2},{7,3},{8,4},{9,5},{1... | collective-permute-start | bytes 786440 | tf_op jit(solution)/shard_map/ppermute | solution.py:27
  79.9 19.5 %collective-permute-start.18 = (bf16[7,128,256]{2,1,0:T(8,128)(2,1)S(1)}, bf16[7,128,256]{2,1,0:T(8,128)(2,1)S(1)}, u32[]{:S(2)}, u32[]{:S(2)}) collective-permute-start(bf16[7,128,256]{2,1,0:T(8,128)(2,1)S(1)} %get-tuple-element.32), channel_id=1, source_target_pairs={{0,1},{1,0},{2,3},{3,2},{4,5},{5,4},{6,7},{7,6},{8,9},{9,8},{10,11... | collective-permute-start | bytes 1376264 | tf_op jit(solution)/shard_map/ppermute | solution.py:27
  82.5 10.2 %collective-permute-start.10 = (bf16[512,256]{1,0:T(8,128)(2,1)S(1)}, bf16[512,256]{1,0:T(8,128)(2,1)S(1)}, u32[]{:S(2)}, u32[]{:S(2)}) collective-permute-start(bf16[512,256]{1,0:T(8,128)(2,1)S(1)} %collective-permute-done.9.refs_2_), channel_id=1, source_target_pairs={{0,4},{1,5},{2,6},{3,7},{4,8},{5,9},{6,10},{7,11},{8,12},{9,13},{1... | collective-permute-start | bytes 786440 | tf_op jit(solution)/shard_map/ppermute | solution.py:27
  85.5 15.3 %collective-permute-start.19 = (bf16[4,128,256]{2,1,0:T(8,128)(2,1)S(1)}, bf16[4,128,256]{2,1,0:T(8,128)(2,1)S(1)}, u32[]{:S(2)}, u32[]{:S(2)}) collective-permute-start(bf16[4,128,256]{2,1,0:T(8,128)(2,1)S(1)} %get-tuple-element.34), channel_id=1, source_target_pairs={{0,1},{1,0},{2,3},{3,2},{4,5},{5,4},{6,7},{7,6},{8,9},{9,8},{10,11... | collective-permute-start | bytes 786440 | tf_op jit(solution)/shard_map/ppermute | solution.py:27
  93.5 9.3 %copy-start.2 = (bf16[1,128,256]{2,1,0:T(8,128)(2,1)}, bf16[1,128,256]{2,1,0:T(8,128)(2,1)S(1)}, u32[]{:S(2)}) copy-start(bf16[1,128,256]{2,1,0:T(8,128)(2,1)S(1)} %get-tuple-element.29.mine_ref) | copy-start | bytes 196612
  93.5 12.6 %collective-permute-start.16 = (f32[256,128]{1,0:T(8,128)S(1)}, f32[256,128]{1,0:T(8,128)S(1)}, u32[]{:S(2)}, u32[]{:S(2)}) collective-permute-start(f32[256,128]{1,0:T(8,128)S(1)} %get-tuple-element.26), channel_id=1, source_target_pairs={{0,1},{1,0},{2,3},{3,2},{4,5},{5,4},{6,7},{7,6},{8,9},{9,8},{10,11... | collective-permute-start | bytes 393224 | tf_op jit(solution)/shard_map/ppermute | solution.py:27
  96.9 6.4 %collective-permute-start.17 = (bf16[1,128,256]{2,1,0:T(8,128)(2,1)S(1)}, bf16[1,128,256]{2,1,0:T(8,128)(2,1)S(1)}, u32[]{:S(2)}, u32[]{:S(2)}) collective-permute-start(bf16[1,128,256]{2,1,0:T(8,128)(2,1)S(1)} %get-tuple-element.30), channel_id=1, source_target_pairs={{0,1},{1,0},{2,3},{3,2},{4,5},{5,4},{6,7},{7,6},{8,9},{9,8},{10,11... | collective-permute-start | bytes 196616 | tf_op jit(solution)/shard_map/ppermute | solution.py:27
  103.3 0.6 copy-start.5

commit v3 on v0

v3 whole, which is shorter than its diff:
```python
import functools

import jax
import jax.numpy as jnp
from jax import lax
from jax.experimental import pallas as pl
from jax.experimental.pallas import tpu as pltpu
from jax.sharding import PartitionSpec as P

TAPS = 3
SECTIONS = 16
NZ = 12
NY = 4
SEQ = 256
LANES = 128
VMEM_LIMIT = 48 * 1024 * 1024

PAIR = 2 * LANES
EARLY = ((0, -1, 1, -2, 2, -3, 3), (-4, 4, -5, 5))
LAST = (-6,)
EXTRA = 2


def along(block, move):
    route = []
    for i in range(NZ * NY):
        z, y = move(i // NY, i % NY)
        route.append((i, (z % NZ) * NY + y))
    return lax.ppermute(block, "fsdp", route)


def from_next_section(block, flip):
    total = NZ * NY
    route = []
    for s in range(SECTIONS):
        for i in range(total):
            source = ((s + 1) % SECTIONS) * total + (i ^ flip)
            route.append((source, s * total + i))
    return lax.ppermute(block, ("section", "fsdp"), route)


def delayed(values, offset):
    rows = lax.broadcasted_iota(jnp.int32, values.shape, 0)
    return jnp.where(rows >= offset, pltpu.roll(values, offset, 0), 0.0)


def advanced(values, offset):
    length = values.shape[0]
    rows = lax.broadcasted_iota(jnp.int32, values.shape, 0)
    shifted = pltpu.roll(values, lax.rem(length - offset, length), 0)
    return jnp.where(rows < length - offset, shifted, 0.0)


def pack_kernel(*refs):
    for i in range(4):
        row, column = (i // 2) * SEQ, (i % 2) * LANES
        refs[4][row : row + SEQ, column : column + LANES] = refs[i][...]


def pack(earlier, earlier_other, received, received_other):
    whole = pl.BlockSpec(memory_space=pltpu.VMEM)
    return pl.pallas_call(
        pack_kernel,
        out_shape=jax.ShapeDtypeStruct((2 * SEQ, PAIR), jnp.bfloat16),
        in_specs=[whole] * 4,
        out_specs=whole,
        compiler_params=pltpu.CompilerParams(vmem_limit_bytes=VMEM_LIMIT),
        name="pack",
    )(earlier, earlier_other, received, received_other)


def columns_of(z, y):
    return pl.ds(pl.multiple_of((z * NY + y) * LANES, LANES), LANES)


def prepare_kernel(place_ref, spacing_ref, saved_ref, taps_ref, weight_ref, keep_ref, send_ref):
    y, spacing = place_ref[1], spacing_ref[0]
    for slot, batch in ((0, 1), (1, 0)):
        values = saved_ref[batch].astype(jnp.float32)
        conv = taps_ref[0, 0:1, :] * values
        for tap in range(1, TAPS):
            conv = conv + taps_ref[0, tap : tap + 1, :] * delayed(values, tap * spacing)
        rows = conv.T.astype(jnp.bfloat16)
        keep_ref[NZ + slot] = rows
        send_ref[NZ + slot] = rows
    for z in range(NZ):
        for flip, lanes in ((0, slice(0, LANES)), (2, slice(LANES, PAIR))):
            keep_ref[z, :, lanes] = weight_ref[:, columns_of(z, y ^ flip)]
            send_ref[z, :, lanes] = weight_ref[:, columns_of(z, y ^ (flip + 1))]


def prepare(place, spacing, saved, taps, weight):
    out = jax.ShapeDtypeStruct((NZ + EXTRA, LANES, PAIR), jnp.bfloat16)
    return call(prepare_kernel, "prepare", (out, out), (place, spacing), (saved, taps, weight))


def call(kernel, name, outs, scalars, arrays, flops=0):
    whole, scalar = pl.BlockSpec(memory_space=pltpu.VMEM), pl.BlockSpec(memory_space=pltpu.SMEM)
    return pl.pallas_call(
        kernel,
        out_shape=outs,
        in_specs=[scalar] * len(scalars) + [whole] * len(arrays),
        out_specs=(whole,) * len(outs),
        compiler_params=pltpu.CompilerParams(vmem_limit_bytes=VMEM_LIMIT),
        cost_estimate=pl.CostEstimate(flops=flops, bytes_accessed=1 << 20, transcendentals=0),
        name=name,
    )(*scalars, *arrays)


def products_kernel(places, last, place_ref, keep_ref, got_ref, *refs):
    blocks, refs = refs[: len(places)], refs[len(places) :]
    had_refs, (mine_ref, theirs_ref, back_ref) = refs[:-3], refs[-3:]
    left = jnp.concatenate(
        [jnp.concatenate([ref[NZ], ref[NZ + 1]], axis=1) for ref in (keep_ref, got_ref)], axis=0
    )
    back = had_refs[0][...] if had_refs else jnp.zeros((SEQ, PAIR), jnp.float32)
    for i, place in enumerate(places):
        block = blocks[i][...]
        grad = jnp.dot(left, block, preferred_element_type=jnp.float32)
        mine_ref[i] = grad[:LANES].astype(jnp.bfloat16)
        theirs_ref[i] = grad[LANES:].astype(jnp.bfloat16)
        at = lax.rem(place_ref[0] + (place + NZ), NZ)
        weight = jnp.concatenate([keep_ref[at], got_ref[at]], axis=0)
        back = back + lax.dot_general(
            block[SEQ:], weight, (((1,), (1,)), ((), ())), preferred_element_type=jnp.float32
        )
    if last:
        other = back[:, LANES:]
        high = other.astype(jnp.bfloat16)
        low = (other - high.astype(jnp.float32)).astype(jnp.bfloat16)
        for i, part in enumerate((high, low)):
            theirs_ref[len(places) + i] = jnp.concatenate([part[:LANES], part[LANES:]], axis=1)
        back_ref[...] = back[:, :LANES]
    else:
        back_ref[...] = back


def products(places, last, place, arrays):
    count = len(places)
    outs = (
        jax.ShapeDtypeStruct((count, LANES, PAIR), jnp.bfloat16),
        jax.ShapeDtypeStruct((count + (EXTRA if last else 0), LANES, PAIR), jnp.bfloat16),
        jax.ShapeDtypeStruct((SEQ, LANES if last else PAIR), jnp.float32),
    )
    flops = 4 * count * PAIR * 2 * SEQ * PAIR
    return call(functools.partial(products_kernel, places, last), "products", outs, (place,), arrays, flops)


def put(out_ref, z, y, source, flip):
    out_ref[:, columns_of(z, y ^ flip)] = source[:, :LANES]
    out_ref[:, columns_of(z, y ^ (flip + 2))] = source[:, LANES:]


def finish_kernel(place_ref, spacing_ref, received_ref, saved_ref, taps_ref, back_ref, *refs):
    pieces, (input_ref, taps_out_ref, out_ref) = refs[:-3], refs[-3:]
    z, y, spacing = place_ref[0], place_ref[1], spacing_ref[0]
    last = pieces[-1]
    parts = [last[len(LAST) + i].astype(jnp.float32) for i in range(EXTRA)]
    total = parts[0] + parts[1]
    back = back_ref[...] + jnp.concatenate([total[:, :LANES], total[:, LANES:]], axis=0)
    values = saved_ref[0].astype(jnp.float32)
    adjoint = received_ref[...].astype(jnp.float32)
    for tap in range(TAPS):
        offset = tap * spacing
        adjoint = adjoint + taps_ref[0, tap : tap + 1, :] * advanced(back, offset)
        taps_out_ref[0, tap : tap + 1, :] = jnp.sum(back * delayed(values, offset), axis=0, keepdims=True)
    input_ref[...] = adjoint.astype(jnp.bfloat16)
    for number, places in enumerate((*EARLY, LAST)):
        for i, place in enumerate(places):
            at = lax.rem(z + (place + NZ), NZ)
            put(out_ref, at, y, pieces[number][i], 0)
            put(out_ref, at, y, pieces[len(EARLY) + 1 + number][i], 1)


def per_device(saved_input, incoming, earlier_grad, w_out, kernel, dilation):
    saved, weight = saved_input[0], w_out[0]
    earlier = earlier_grad[0]
    index = lax.axis_index("fsdp")
    place = jnp.stack([lax.div(index, NY), lax.rem(index, NY)]).astype(jnp.int32)
    partner = lambda z, y: (z, y ^ 1)

    received = from_next_section(incoming[0], 0)
    received_other = from_next_section(incoming[0], 2)
    earlier_other = along(earlier, lambda z, y: (z, y ^ 2))
    keep, send = prepare(place, dilation, saved, kernel, weight)
    ring, back, mine, other = {0: pack(earlier, earlier_other, received, received_other)}, (), [], []
    for step in range(1, NZ // 2 + 1):
        if step == 2:
            ring[-1], ring[1], keep, send = lax.optimization_barrier((ring[-1], ring[1], keep, send))
            got = along(send, partner)
        if step == 5:
            one, two, *back = products(EARLY[0], False, place, (keep, got, *(ring[p] for p in EARLY[0])))
            mine.append(one)
            ring[1 - step], two = lax.optimization_barrier((ring[1 - step], two))
            other.append(along(two, partner))
        ring[-step] = along(ring[1 - step], lambda z, y: (z + 1, y))
        if step < NZ // 2:
            ring[step] = along(ring[step - 1], lambda z, y: (z - 1, y))
    one, two, *back = products(EARLY[1], False, place, (keep, got, *(ring[p] for p in EARLY[1]), *back))
    mine.append(one)
    other.append(along(two, partner))
    ring[LAST[0]], other[0] = lax.optimization_barrier((ring[LAST[0]], other[0]))
    one, two, back = products(LAST, True, place, (keep, got, *(ring[p] for p in LAST), *back))
    mine.append(one)
    other.append(along(two, partner))
    outs = (
        jax.ShapeDtypeStruct((SEQ, LANES), jnp.bfloat16),
        jax.ShapeDtypeStruct((1, TAPS, LANES), jnp.float32),
        jax.ShapeDtypeStruct((LANES, NZ * NY * LANES), jnp.bfloat16),
    )
    grad_input, grad_kernel, grad_weight = call(
        finish_kernel, "finish", outs, (place, dilation), (received, saved, kernel, back, *mine, *other)
    )
    return grad_input[None], grad_kernel, grad_weight[None]


def solution(mesh):
    return jax.shard_map(
        per_device,
        mesh=mesh,
        in_specs=(
            P("section", None, None, "fsdp"),
            P("section", None, "fsdp"),
            P("section", None, "fsdp"),
            P("section", "fsdp", None),
            P("section", None, "fsdp"),
            P("section"),
        ),
        out_specs=(
            P("section", None, "fsdp"),
            P("section", None, "fsdp"),
            P("section", "fsdp", None),
        ),
        check_vma=False,
    )
```

time: 437 us -> 107 us (0.24)
  waiting for transfers between devices: 404 us -> 25.9 us
  starting transfers between devices: 2.25 us -> 67.8 us
  between operations: 14.8 us -> 1.55 us
  matrix products: 10.9 us -> 0 us
  Pallas kernels: 0 us -> 6.81 us
    all_gather x2 -> x0, waiting for transfers between devices: 401 us -> none  [the longest x1 204 us: per_device(): lax.all_gather(earlier_grad, 'fsdp', axis=2, tiled=True)[0]]
    ppermute x1 -> x18, starting transfers between devices: 2.18 us -> 67.8 us  [the longest x16 63.6 us: along(): return lax.ppermute(block, 'fsdp', route)]
    ppermute x1 -> x18, waiting for transfers between devices: 2.2 us -> 25.9 us  [the longest x16 23 us: along(): return lax.ppermute(block, 'fsdp', route)]
    dot_general x3 -> x0, matrix products: 10.9 us -> none  [the longest x2 7.93 us: steps_by_steps(): lax.dot_general(left, right, (((0,), (0,)), ((), ())), preferred_element_...]
    pallas_call x0 -> x6, Pallas kernels: none -> 6.81 us  [the longest x5 6.77 us: call(): pl.pallas_call(kernel, out_shape=outs, in_specs=[scalar] * len(scalars) +...]
  transfers between devices with their start and end apart: 3 -> 18, of which waited for: 3 -> 10; matrix products, arithmetic and copies ran while one was open for 1% -> 1% of each run, Pallas kernels for 0% -> 4%
where the time goes in v3:
time: 107 us
  starting transfers between devices  67.8 us (63%)
  waiting for transfers between devices  25.9 us (24%)
  Pallas kernels  6.81 us (6%)
  local copies, waits for them, and re-layouts  4.4 us (4%)
  between operations  1.55 us (1%)
    ppermute x16, starting transfers between devices, along(): return lax.ppermute(block, 'fsdp', route)  63.6 us
    ppermute x16, waiting for transfers between devices, along(): return lax.ppermute(block, 'fsdp', route)  23 us
    pallas_call x5, Pallas kernels, call(): pl.pallas_call(kernel, out_shape=outs, in_specs=[scalar] * len(scalars) +...  6.77 us
    unnamed x10, local copies, waits for them, and re-layouts  4.4 us
    ppermute x2, starting transfers between devices, from_next_section(): return lax.ppermute(block, ('section', 'fsdp'), route)  4.25 us
    ppermute x2, waiting for transfers between devices, from_next_section(): return lax.ppermute(block, ('section', 'fsdp'), route)  2.92 us
  transfers between devices with their start and end apart: 18, of which 10 were waited for; matrix products, arithmetic and copies ran while one was open for 1% of the time, Pallas kernels for 4%

profile of v3, /device:TPU:6, one launch (start us, length us, event | category | flops | bytes accessed | tf_op | source)
XLA Modules:
  0.0 106.6 jit_solution(16054518015787921063)
XLA Ops:
  0.6 2.2 %collective-permute-start = (bf16[256,128]{1,0:T(8,128)(2,1)}, bf16[256,128]{1,0:T(8,128)(2,1)S(1)}, u32[]{:S(2)}, u32[]{:S(2)}) collective-permute-start(bf16[256,128]{1,0:T(8,128)(2,1)} %bitcast.14), channel_id=1, source_target_pairs={{48,0},{49,1},{50,2},{51,3},{52,4},{53,5},{54,6},{55,7},{56,8},{57... | collective-permute-start | bytes 196616 | tf_op jit(solution)/shard_map/ppermute | solution.py:39
  2.8 4.5 %collective-permute-start.1 = (bf16[256,128]{1,0:T(8,128)(2,1)}, bf16[256,128]{1,0:T(8,128)(2,1)S(1)}, u32[]{:S(2)}, u32[]{:S(2)}) collective-permute-start(bf16[256,128]{1,0:T(8,128)(2,1)} %bitcast.11), channel_id=1, source_target_pairs={{0,2},{1,3},{2,0},{3,1},{4,6},{5,7},{6,4},{7,5},{8,10},{9,11},{10,... | collective-permute-start | bytes 196616 | tf_op jit(solution)/shard_map/ppermute | solution.py:29
  7.3 2.1 %collective-permute-start.2 = (bf16[256,128]{1,0:T(8,128)(2,1)}, bf16[256,128]{1,0:T(8,128)(2,1)S(1)}, u32[]{:S(2)}, u32[]{:S(2)}) collective-permute-start(bf16[256,128]{1,0:T(8,128)(2,1)} %bitcast.15), channel_id=1, source_target_pairs={{50,0},{51,1},{48,2},{49,3},{54,4},{55,5},{52,6},{53,7},{58,8},{59... | collective-permute-start | bytes 196616 | tf_op jit(solution)/shard_map/ppermute | solution.py:39
  9.4 0.0 collective-permute-done.refs_2_.received_ref
  9.4 2.1 %collective-permute-done.1.refs_1_ = bf16[256,128]{1,0:T(8,128)(2,1)S(1)} collective-permute-done((bf16[256,128]{1,0:T(8,128)(2,1)}, bf16[256,128]{1,0:T(8,128)(2,1)S(1)}, u32[]{:S(2)}, u32[]{:S(2)}) %collective-permute-start.1) | collective-permute-done | bytes 65568 | tf_op jit(solution)/shard_map/ppermute | solution.py:29
  11.5 2.9 %collective-permute-done.2.refs_3_ = bf16[256,128]{1,0:T(8,128)(2,1)S(1)} collective-permute-done((bf16[256,128]{1,0:T(8,128)(2,1)}, bf16[256,128]{1,0:T(8,128)(2,1)S(1)}, u32[]{:S(2)}, u32[]{:S(2)}) %collective-permute-start.2) | collective-permute-done | bytes 65568 | tf_op jit(solution)/shard_map/ppermute | solution.py:39
  14.4 0.8 copy-done.3
  15.3 4.3 %collective-permute-start.3 = (bf16[512,256]{1,0:T(8,128)(2,1)S(1)}, bf16[512,256]{1,0:T(8,128)(2,1)S(1)}, u32[]{:S(2)}, u32[]{:S(2)}) collective-permute-start(bf16[512,256]{1,0:T(8,128)(2,1)S(1)} %pack.1.refs_0_), channel_id=1, source_target_pairs={{0,4},{1,5},{2,6},{3,7},{4,8},{5,9},{6,10},{7,11},{8,12},{9,13},{1... | collective-permute-start | bytes 786440 | tf_op jit(solution)/shard_map/ppermute | solution.py:29
  19.6 12.2 %collective-permute-start.4 = (bf16[512,256]{1,0:T(8,128)(2,1)S(1)}, bf16[512,256]{1,0:T(8,128)(2,1)S(1)}, u32[]{:S(2)}, u32[]{:S(2)}) collective-permute-start(bf16[512,256]{1,0:T(8,128)(2,1)S(1)} %pack.1.refs_0_), channel_id=1, source_target_pairs={{0,44},{1,45},{2,46},{3,47},{4,0},{5,1},{6,2},{7,3},{8,4},{9,5},{1... | collective-permute-start | bytes 786440 | tf_op jit(solution)/shard_map/ppermute | solution.py:29
  31.8 0.7 copy.10.taps_ref
  33.2 0.1 pad_add_fusion.place_ref
  33.2 1.4 %copy-done = bf16[1,128,6144]{2,1,0:T(8,128)(2,1)S(1)} copy-done((bf16[1,128,6144]{2,1,0:T(8,128)(2,1)S(1)}, bf16[1,128,6144]{2,1,0:T(8,128)(2,1)}, u32[]{:S(2)}) %copy-start) | copy-done | bytes 1572888
  34.7 0.9 copy-done.1
  35.6 1.2 %prepare.1 = (bf16[14,128,256]{2,1,0:T(8,128)(2,1)S(1)}, bf16[14,128,256]{2,1,0:T(8,128)(2,1)S(1)}) custom-call(s32[2]{0:T(128)S(1)} %pad_add_fusion.place_ref, s32[1]{0:T(128)S(6)} %copy.12.spacing_ref, bf16[2,256,128]{2,1,0:T(8,128)(2,1)S(1)} %bitcast.9, f32[1,3,128]{2,1,0:T(4,128)S(1)} %copy.10.taps_ref, bf16[128,6144]{1,0:T(8,128)(2,1)S(1)} %bitcast.8), custom_call_target="tpu_custom_call" | custom-call | bytes 1048576 | tf_op jit(solution)/shard_map/prepare/pallas_call | solution.py:99
  36.7 0.0 collective-permute-done.3.refs_1_
  36.8 0.0 collective-permute-done.4.refs_2_
  36.8 3.6 %collective-permute-start.5 = (bf16[14,128,256]{2,1,0:T(8,128)(2,1)S(1)}, bf16[14,128,256]{2,1,0:T(8,128)(2,1)S(1)}, u32[]{:S(2)}, u32[]{:S(2)}) collective-permute-start(bf16[14,128,256]{2,1,0:T(8,128)(2,1)S(1)} %get-tuple-element.28), channel_id=1, source_target_pairs={{0,1},{1,0},{2,3},{3,2},{4,5},{5,4},{6,7},{7,6},{8,9},{9,8},{10,11... | collective-permute-start | bytes 2752520 | tf_op jit(solution)/shard_map/ppermute | solution.py:29
  40.3 1.9 %collective-permute-start.6 = (bf16[512,256]{1,0:T(8,128)(2,1)S(1)}, bf16[512,256]{1,0:T(8,128)(2,1)S(1)}, u32[]{:S(2)}, u32[]{:S(2)}) collective-permute-start(bf16[512,256]{1,0:T(8,128)(2,1)S(1)} %collective-permute-done.3.refs_1_), channel_id=1, source_target_pairs={{0,4},{1,5},{2,6},{3,7},{4,8},{5,9},{6,10},{7,11},{8,12},{9,13},{1... | collective-permute-start | bytes 786440 | tf_op jit(solution)/shard_map/ppermute | solution.py:29
  42.3 5.1 %collective-permute-start.9 = (bf16[512,256]{1,0:T(8,128)(2,1)S(1)}, bf16[512,256]{1,0:T(8,128)(2,1)S(1)}, u32[]{:S(2)}, u32[]{:S(2)}) collective-permute-start(bf16[512,256]{1,0:T(8,128)(2,1)S(1)} %collective-permute-done.4.refs_2_), channel_id=1, source_target_pairs={{0,44},{1,45},{2,46},{3,47},{4,0},{5,1},{6,2},{7,3},{8,4},{9,5},{1... | collective-permute-start | bytes 786440 | tf_op jit(solution)/shard_map/ppermute | solution.py:29
  47.4 3.3 %collective-permute-done.6.refs_3_ = bf16[512,256]{1,0:T(8,128)(2,1)S(1)} collective-permute-done((bf16[512,256]{1,0:T(8,128)(2,1)S(1)}, bf16[512,256]{1,0:T(8,128)(2,1)S(1)}, u32[]{:S(2)}, u32[]{:S(2)}) %collective-permute-start.6) | collective-permute-done | bytes 262176 | tf_op jit(solution)/shard_map/ppermute | solution.py:29
  50.7 1.9 %collective-permute-start.7 = (bf16[512,256]{1,0:T(8,128)(2,1)S(1)}, bf16[512,256]{1,0:T(8,128)(2,1)S(1)}, u32[]{:S(2)}, u32[]{:S(2)}) collective-permute-start(bf16[512,256]{1,0:T(8,128)(2,1)S(1)} %collective-permute-done.6.refs_3_), channel_id=1, source_target_pairs={{0,4},{1,5},{2,6},{3,7},{4,8},{5,9},{6,10},{7,11},{8,12},{9,13},{1... | collective-permute-start | bytes 786440 | tf_op jit(solution)/shard_map/ppermute | solution.py:29
  52.6 0.0 collective-permute-done.9.refs_4_
  52.6 5.4 %collective-permute-start.10 = (bf16[512,256]{1,0:T(8,128)(2,1)S(1)}, bf16[512,256]{1,0:T(8,128)(2,1)S(1)}, u32[]{:S(2)}, u32[]{:S(2)}) collective-permute-start(bf16[512,256]{1,0:T(8,128)(2,1)S(1)} %collective-permute-done.9.refs_4_), channel_id=1, source_target_pairs={{0,44},{1,45},{2,46},{3,47},{4,0},{5,1},{6,2},{7,3},{8,4},{9,5},{1... | collective-permute-start | bytes 786440 | tf_op jit(solution)/shard_map/ppermute | solution.py:29
  58.0 4.2 %collective-permute-done.7.refs_5_ = bf16[512,256]{1,0:T(8,128)(2,1)S(1)} collective-permute-done((bf16[512,256]{1,0:T(8,128)(2,1)S(1)}, bf16[512,256]{1,0:T(8,128)(2,1)S(1)}, u32[]{:S(2)}, u32[]{:S(2)}) %collective-permute-start.7) | collective-permute-done | bytes 262176 | tf_op jit(solution)/shard_map/ppermute | solution.py:29
  62.2 1.9 %collective-permute-start.8 = (bf16[512,256]{1,0:T(8,128)(2,1)S(1)}, bf16[512,256]{1,0:T(8,128)(2,1)S(1)}, u32[]{:S(2)}, u32[]{:S(2)}) collective-permute-start(bf16[512,256]{1,0:T(8,128)(2,1)S(1)} %collective-permute-done.7.refs_5_), channel_id=1, source_target_pairs={{0,4},{1,5},{2,6},{3,7},{4,8},{5,9},{6,10},{7,11},{8,12},{9,13},{1... | collective-permute-start | bytes 786440 | tf_op jit(solution)/shard_map/ppermute | solution.py:29
  64.1 0.1 collective-permute-done.10.refs_6_
  64.3 5.6 %collective-permute-start.14 = (bf16[512,256]{1,0:T(8,128)(2,1)S(1)}, bf16[512,256]{1,0:T(8,128)(2,1)S(1)}, u32[]{:S(2)}, u32[]{:S(2)}) collective-permute-start(bf16[512,256]{1,0:T(8,128)(2,1)S(1)} %collective-permute-done.10.refs_6_), channel_id=1, source_target_pairs={{0,44},{1,45},{2,46},{3,47},{4,0},{5,1},{6,2},{7,3},{8,4},{9,5},{1... | collective-permute-start | bytes 786440 | tf_op jit(solution)/shard_map/ppermute | solution.py:29
  69.9 0.0 collective-permute-done.5.got_ref
  69.9 1.4 %products.3 = (bf16[7,128,256]{2,1,0:T(8,128)(2,1)S(1)}, bf16[7,128,256]{2,1,0:T(8,128)(2,1)S(1)}, f32[256,256]{1,0:T(8,128)S(1)}) custom-call(s32[2]{0:T(128)S(1)} %pad_add_fusion.place_ref, bf16[14,128,256]{2,1,0:T(8,128)(2,1)S(1)} %get-tuple-element.27.keep_ref, bf16[14,128,256]{2,1,0:T(8,128)(2,1)S(1)} %collective-permute-done.5.got_ref, ...), custom_call_target="tpu_custom_call" | custom-call | flops 939524096 | bytes 1048576 | tf_op jit(solution)/shard_map/products/pallas_call | solution.py:99
  71.3 2.8 %collective-permute-done.8.refs_0_ = bf16[512,256]{1,0:T(8,128)(2,1)S(1)} collective-permute-done((bf16[512,256]{1,0:T(8,128)(2,1)S(1)}, bf16[512,256]{1,0:T(8,128)(2,1)S(1)}, u32[]{:S(2)}, u32[]{:S(2)}) %collective-permute-start.8) | collective-permute-done | bytes 262176 | tf_op jit(solution)/shard_map/ppermute | solution.py:29
  74.1 1.9 %collective-permute-start.11 = (bf16[512,256]{1,0:T(8,128)(2,1)S(1)}, bf16[512,256]{1,0:T(8,128)(2,1)S(1)}, u32[]{:S(2)}, u32[]{:S(2)}) collective-permute-start(bf16[512,256]{1,0:T(8,128)(2,1)S(1)} %collective-permute-done.8.refs_0_), channel_id=1, source_target_pairs={{0,4},{1,5},{2,6},{3,7},{4,8},{5,9},{6,10},{7,11},{8,12},{9,13},{1... | collective-permute-start | bytes 786440 | tf_op jit(solution)/shard_map/ppermute | solution.py:29
  76.0 2.1 %collective-permute-start.13 = (bf16[7,128,256]{2,1,0:T(8,128)(2,1)S(1)}, bf16[7,128,256]{2,1,0:T(8,128)(2,1)S(1)}, u32[]{:S(2)}, u32[]{:S(2)}) collective-permute-start(bf16[7,128,256]{2,1,0:T(8,128)(2,1)S(1)} %get-tuple-element.33), channel_id=1, source_target_pairs={{0,1},{1,0},{2,3},{3,2},{4,5},{5,4},{6,7},{7,6},{8,9},{9,8},{10,11... | collective-permute-start | bytes 1376264 | tf_op jit(solution)/shard_map/ppermute | solution.py:29
  78.1 0.0 collective-permute-done.14.refs_1_
  78.1 5.1 %collective-permute-start.15 = (bf16[512,256]{1,0:T(8,128)(2,1)S(1)}, bf16[512,256]{1,0:T(8,128)(2,1)S(1)}, u32[]{:S(2)}, u32[]{:S(2)}) collective-permute-start(bf16[512,256]{1,0:T(8,128)(2,1)S(1)} %collective-permute-done.14.refs_1_), channel_id=1, source_target_pairs={{0,44},{1,45},{2,46},{3,47},{4,0},{5,1},{6,2},{7,3},{8,4},{9,5},{1... | collective-permute-start | bytes 786440 | tf_op jit(solution)/shard_map/ppermute | solution.py:29
  83.3 1.9 %collective-permute-done.11.refs_2_ = bf16[512,256]{1,0:T(8,128)(2,1)S(1)} collective-permute-done((bf16[512,256]{1,0:T(8,128)(2,1)S(1)}, bf16[512,256]{1,0:T(8,128)(2,1)S(1)}, u32[]{:S(2)}, u32[]{:S(2)}) %collective-permute-start.11) | collective-permute-done | bytes 262176 | tf_op jit(solution)/shard_map/ppermute | solution.py:29
  85.2 1.9 %collective-permute-start.12 = (bf16[512,256]{1,0:T(8,128)(2,1)S(1)}, bf16[512,256]{1,0:T(8,128)(2,1)S(1)}, u32[]{:S(2)}, u32[]{:S(2)}) collective-permute-start(bf16[512,256]{1,0:T(8,128)(2,1)S(1)} %collective-permute-done.11.refs_2_), channel_id=1, source_target_pairs={{0,4},{1,5},{2,6},{3,7},{4,8},{5,9},{6,10},{7,11},{8,12},{9,13},{1... | collective-permute-start | bytes 786440 | tf_op jit(solution)/shard_map/ppermute | solution.py:29
  87.1 1.2 %collective-permute-done.15.refs_3_ = bf16[512,256]{1,0:T(8,128)(2,1)S(1)} collective-permute-done((bf16[512,256]{1,0:T(8,128)(2,1)S(1)}, bf16[512,256]{1,0:T(8,128)(2,1)S(1)}, u32[]{:S(2)}, u32[]{:S(2)}) %collective-permute-start.15) | collective-permute-done | bytes 262176 | tf_op jit(solution)/shard_map/ppermute | solution.py:29
  88.3 1.1 %products.4 = (bf16[4,128,256]{2,1,0:T(8,128)(2,1)S(1)}, bf16[4,128,256]{2,1,0:T(8,128)(2,1)S(1)}, f32[256,256]{1,0:T(8,128)S(1)}) custom-call(s32[2]{0:T(128)S(1)} %pad_add_fusion.place_ref, bf16[14,128,256]{2,1,0:T(8,128)(2,1)S(1)} %get-tuple-element.27.keep_ref, bf16[14,128,256]{2,1,0:T(8,128)(2,1)S(1)} %collective-permute-done.5.got_ref, ...), custom_call_target="tpu_custom_call" | custom-call | flops 536870912 | bytes 1048576 | tf_op jit(solution)/shard_map/products/pallas_call | solution.py:99
  89.5 0.0 copy-start.2
  89.5 3.8 %collective-permute-start.16 = (bf16[4,128,256]{2,1,0:T(8,128)(2,1)S(1)}, bf16[4,128,256]{2,1,0:T(8,128)(2,1)S(1)}, u32[]{:S(2)}, u32[]{:S(2)}) collective-permute-start(bf16[4,128,256]{2,1,0:T(8,128)(2,1)S(1)} %get-tuple-element.42), channel_id=1, source_target_pairs={{0,1},{1,0},{2,3},{3,2},{4,5},{5,4},{6,7},{7,6},{8,9},{9,8},{10,11... | collective-permute-start | bytes 786440 | tf_op jit(solution)/shard_map/ppermute | solution.py:29
  93.3 0.0 collective-permute-done.13.refs_3_
  93.3 2.2 %collective-permute-done.12.refs_0_ = bf16[512,256]{1,0:T(8,128)(2,1)S(1)} collective-permute-done((bf16[512,256]{1,0:T(8,128)(2,1)S(1)}, bf16[512,256]{1,0:T(8,128)(2,1)S(1)}, u32[]{:S(2)}, u32[]{:S(2)}) %collective-permute-start.12) | collective-permute-done | bytes 262176 | tf_op jit(solution)/shard_map/ppermute | solution.py:29
  95.4 0.8 products.5
  96.3 2.3 %collective-permute-start.17 = (bf16[3,128,256]{2,1,0:T(8,128)(2,1)S(1)}, bf16[3,128,256]{2,1,0:T(8,128)(2,1)S(1)}, u32[]{:S(2)}, u32[]{:S(2)}) collective-permute-start(bf16[3,128,256]{2,1,0:T(8,128)(2,1)S(1)} %get-tuple-element.43), channel_id=1, source_target_pairs={{0,1},{1,0},{2,3},{3,2},{4,5},{5,4},{6,7},{7,6},{8,9},{9,8},{10,11... | collective-permute-start | bytes 589832 | tf_op jit(solution)/shard_map/ppermute | solution.py:29
  98.6 0.0 collective-permute-done.16.refs_4_
  98.6 5.2 %collective-permute-done.17.refs_5_ = bf16[3,128,256]{2,1,0:T(8,128)(2,1)S(1)} collective-permute-done((bf16[3,128,256]{2,1,0:T(8,128)(2,1)S(1)}, bf16[3,128,256]{2,1,0:T(8,128)(2,1)S(1)}, u32[]{:S(2)}, u32[]{:S(2)}) %collective-permute-start.17) | collective-permute-done | bytes 196640 | tf_op jit(solution)/shard_map/ppermute | solution.py:29
  103.8 2.2 %finish.1 = (bf16[256,128]{1,0:T(8,128)(2,1)}, f32[1,3,128]{2,1,0:T(4,128)S(1)}, bf16[128,6144]{1,0:T(8,128)(2,1)}) custom-call(s32[2]{0:T(128)S(1)} %pad_add_fusion.place_ref, s32[1]{0:T(128)S(6)} %copy.12.spacing_ref, bf16[256,128]{1,0:T(8,128)(2,1)S(1)} %collective-permute-done.refs_2_.received_ref, bf16[2,256,128]{2,1,0:T(8,128)(2,1)S(1)} %bitcast.10, ...), custom_call_target="tpu_custom_call" | custom-call | bytes 1048576 | tf_op jit(solution)/shard_map/finish/pallas_call | solution.py:99
  106.0 0.6 copy.11
  (5 shorter events, 0.1 us)
Async XLA Ops:
  0.6 8.8 %collective-permute-start = (bf16[256,128]{1,0:T(8,128)(2,1)}, bf16[256,128]{1,0:T(8,128)(2,1)S(1)}, u32[]{:S(2)}, u32[]{:S(2)}) collective-permute-start(bf16[256,128]{1,0:T(8,128)(2,1)} %bitcast.14), channel_id=1, source_target_pairs={{48,0},{49,1},{50,2},{51,3},{52,4},{53,5},{54,6},{55,7},{56,8},{57... | collective-permute-start | bytes 196616 | tf_op jit(solution)/shard_map/ppermute | solution.py:39
  2.8 8.7 %collective-permute-start.1 = (bf16[256,128]{1,0:T(8,128)(2,1)}, bf16[256,128]{1,0:T(8,128)(2,1)S(1)}, u32[]{:S(2)}, u32[]{:S(2)}) collective-permute-start(bf16[256,128]{1,0:T(8,128)(2,1)} %bitcast.11), channel_id=1, source_target_pairs={{0,2},{1,3},{2,0},{3,1},{4,6},{5,7},{6,4},{7,5},{8,10},{9,11},{10,... | collective-permute-start | bytes 196616 | tf_op jit(solution)/shard_map/ppermute | solution.py:29
  7.3 7.1 %collective-permute-start.2 = (bf16[256,128]{1,0:T(8,128)(2,1)}, bf16[256,128]{1,0:T(8,128)(2,1)S(1)}, u32[]{:S(2)}, u32[]{:S(2)}) collective-permute-start(bf16[256,128]{1,0:T(8,128)(2,1)} %bitcast.15), channel_id=1, source_target_pairs={{50,0},{51,1},{48,2},{49,3},{54,4},{55,5},{52,6},{53,7},{58,8},{59... | collective-permute-start | bytes 196616 | tf_op jit(solution)/shard_map/ppermute | solution.py:39
  14.4 0.8 copy-start.3
  15.3 21.5 %collective-permute-start.3 = (bf16[512,256]{1,0:T(8,128)(2,1)S(1)}, bf16[512,256]{1,0:T(8,128)(2,1)S(1)}, u32[]{:S(2)}, u32[]{:S(2)}) collective-permute-start(bf16[512,256]{1,0:T(8,128)(2,1)S(1)} %pack.1.refs_0_), channel_id=1, source_target_pairs={{0,4},{1,5},{2,6},{3,7},{4,8},{5,9},{6,10},{7,11},{8,12},{9,13},{1... | collective-permute-start | bytes 786440 | tf_op jit(solution)/shard_map/ppermute | solution.py:29
  19.6 17.2 %collective-permute-start.4 = (bf16[512,256]{1,0:T(8,128)(2,1)S(1)}, bf16[512,256]{1,0:T(8,128)(2,1)S(1)}, u32[]{:S(2)}, u32[]{:S(2)}) collective-permute-start(bf16[512,256]{1,0:T(8,128)(2,1)S(1)} %pack.1.refs_0_), channel_id=1, source_target_pairs={{0,44},{1,45},{2,46},{3,47},{4,0},{5,1},{6,2},{7,3},{8,4},{9,5},{1... | collective-permute-start | bytes 786440 | tf_op jit(solution)/shard_map/ppermute | solution.py:29
  33.2 1.4 %copy-start = (bf16[1,128,6144]{2,1,0:T(8,128)(2,1)S(1)}, bf16[1,128,6144]{2,1,0:T(8,128)(2,1)}, u32[]{:S(2)}) copy-start(bf16[1,128,6144]{2,1,0:T(8,128)(2,1)} %param.9) | copy-start | bytes 4718596
  34.7 0.9 copy-start.1
  36.8 33.1 %collective-permute-start.5 = (bf16[14,128,256]{2,1,0:T(8,128)(2,1)S(1)}, bf16[14,128,256]{2,1,0:T(8,128)(2,1)S(1)}, u32[]{:S(2)}, u32[]{:S(2)}) collective-permute-start(bf16[14,128,256]{2,1,0:T(8,128)(2,1)S(1)} %get-tuple-element.28), channel_id=1, source_target_pairs={{0,1},{1,0},{2,3},{3,2},{4,5},{5,4},{6,7},{7,6},{8,9},{9,8},{10,11... | collective-permute-start | bytes 2752520 | tf_op jit(solution)/shard_map/ppermute | solution.py:29
  40.3 10.3 %collective-permute-start.6 = (bf16[512,256]{1,0:T(8,128)(2,1)S(1)}, bf16[512,256]{1,0:T(8,128)(2,1)S(1)}, u32[]{:S(2)}, u32[]{:S(2)}) collective-permute-start(bf16[512,256]{1,0:T(8,128)(2,1)S(1)} %collective-permute-done.3.refs_1_), channel_id=1, source_target_pairs={{0,4},{1,5},{2,6},{3,7},{4,8},{5,9},{6,10},{7,11},{8,12},{9,13},{1... | collective-permute-start | bytes 786440 | tf_op jit(solution)/shard_map/ppermute | solution.py:29
  42.3 10.3 %collective-permute-start.9 = (bf16[512,256]{1,0:T(8,128)(2,1)S(1)}, bf16[512,256]{1,0:T(8,128)(2,1)S(1)}, u32[]{:S(2)}, u32[]{:S(2)}) collective-permute-start(bf16[512,256]{1,0:T(8,128)(2,1)S(1)} %collective-permute-done.4.refs_2_), channel_id=1, source_target_pairs={{0,44},{1,45},{2,46},{3,47},{4,0},{5,1},{6,2},{7,3},{8,4},{9,5},{1... | collective-permute-start | bytes 786440 | tf_op jit(solution)/shard_map/ppermute | solution.py:29
  50.7 11.5 %collective-permute-start.7 = (bf16[512,256]{1,0:T(8,128)(2,1)S(1)}, bf16[512,256]{1,0:T(8,128)(2,1)S(1)}, u32[]{:S(2)}, u32[]{:S(2)}) collective-permute-start(bf16[512,256]{1,0:T(8,128)(2,1)S(1)} %collective-permute-done.6.refs_3_), channel_id=1, source_target_pairs={{0,4},{1,5},{2,6},{3,7},{4,8},{5,9},{6,10},{7,11},{8,12},{9,13},{1... | collective-permute-start | bytes 786440 | tf_op jit(solution)/shard_map/ppermute | solution.py:29
  52.6 11.6 %collective-permute-start.10 = (bf16[512,256]{1,0:T(8,128)(2,1)S(1)}, bf16[512,256]{1,0:T(8,128)(2,1)S(1)}, u32[]{:S(2)}, u32[]{:S(2)}) collective-permute-start(bf16[512,256]{1,0:T(8,128)(2,1)S(1)} %collective-permute-done.9.refs_4_), channel_id=1, source_target_pairs={{0,44},{1,45},{2,46},{3,47},{4,0},{5,1},{6,2},{7,3},{8,4},{9,5},{1... | collective-permute-start | bytes 786440 | tf_op jit(solution)/shard_map/ppermute | solution.py:29
  62.2 11.9 %collective-permute-start.8 = (bf16[512,256]{1,0:T(8,128)(2,1)S(1)}, bf16[512,256]{1,0:T(8,128)(2,1)S(1)}, u32[]{:S(2)}, u32[]{:S(2)}) collective-permute-start(bf16[512,256]{1,0:T(8,128)(2,1)S(1)} %collective-permute-done.7.refs_5_), channel_id=1, source_target_pairs={{0,4},{1,5},{2,6},{3,7},{4,8},{5,9},{6,10},{7,11},{8,12},{9,13},{1... | collective-permute-start | bytes 786440 | tf_op jit(solution)/shard_map/ppermute | solution.py:29
  64.3 13.9 %collective-permute-start.14 = (bf16[512,256]{1,0:T(8,128)(2,1)S(1)}, bf16[512,256]{1,0:T(8,128)(2,1)S(1)}, u32[]{:S(2)}, u32[]{:S(2)}) collective-permute-start(bf16[512,256]{1,0:T(8,128)(2,1)S(1)} %collective-permute-done.10.refs_6_), channel_id=1, source_target_pairs={{0,44},{1,45},{2,46},{3,47},{4,0},{5,1},{6,2},{7,3},{8,4},{9,5},{1... | collective-permute-start | bytes 786440 | tf_op jit(solution)/shard_map/ppermute | solution.py:29
  74.1 11.1 %collective-permute-start.11 = (bf16[512,256]{1,0:T(8,128)(2,1)S(1)}, bf16[512,256]{1,0:T(8,128)(2,1)S(1)}, u32[]{:S(2)}, u32[]{:S(2)}) collective-permute-start(bf16[512,256]{1,0:T(8,128)(2,1)S(1)} %collective-permute-done.8.refs_0_), channel_id=1, source_target_pairs={{0,4},{1,5},{2,6},{3,7},{4,8},{5,9},{6,10},{7,11},{8,12},{9,13},{1... | collective-permute-start | bytes 786440 | tf_op jit(solution)/shard_map/ppermute | solution.py:29
  76.0 17.2 %collective-permute-start.13 = (bf16[7,128,256]{2,1,0:T(8,128)(2,1)S(1)}, bf16[7,128,256]{2,1,0:T(8,128)(2,1)S(1)}, u32[]{:S(2)}, u32[]{:S(2)}) collective-permute-start(bf16[7,128,256]{2,1,0:T(8,128)(2,1)S(1)} %get-tuple-element.33), channel_id=1, source_target_pairs={{0,1},{1,0},{2,3},{3,2},{4,5},{5,4},{6,7},{7,6},{8,9},{9,8},{10,11... | collective-permute-start | bytes 1376264 | tf_op jit(solution)/shard_map/ppermute | solution.py:29
  78.1 10.2 %collective-permute-start.15 = (bf16[512,256]{1,0:T(8,128)(2,1)S(1)}, bf16[512,256]{1,0:T(8,128)(2,1)S(1)}, u32[]{:S(2)}, u32[]{:S(2)}) collective-permute-start(bf16[512,256]{1,0:T(8,128)(2,1)S(1)} %collective-permute-done.14.refs_1_), channel_id=1, source_target_pairs={{0,44},{1,45},{2,46},{3,47},{4,0},{5,1},{6,2},{7,3},{8,4},{9,5},{1... | collective-permute-start | bytes 786440 | tf_op jit(solution)/shard_map/ppermute | solution.py:29
  85.2 10.2 %collective-permute-start.12 = (bf16[512,256]{1,0:T(8,128)(2,1)S(1)}, bf16[512,256]{1,0:T(8,128)(2,1)S(1)}, u32[]{:S(2)}, u32[]{:S(2)}) collective-permute-start(bf16[512,256]{1,0:T(8,128)(2,1)S(1)} %collective-permute-done.11.refs_2_), channel_id=1, source_target_pairs={{0,4},{1,5},{2,6},{3,7},{4,8},{5,9},{6,10},{7,11},{8,12},{9,13},{1... | collective-permute-start | bytes 786440 | tf_op jit(solution)/shard_map/ppermute | solution.py:29
  89.5 14.4 %copy-start.2 = (bf16[1,2,256,128]{3,2,1,0:T(8,128)(2,1)S(1)}, bf16[1,2,256,128]{3,2,1,0:T(8,128)(2,1)}, u32[]{:S(2)}) copy-start(bf16[1,2,256,128]{3,2,1,0:T(8,128)(2,1)} %param.6) | copy-start | bytes 393220
  89.5 9.1 %collective-permute-start.16 = (bf16[4,128,256]{2,1,0:T(8,128)(2,1)S(1)}, bf16[4,128,256]{2,1,0:T(8,128)(2,1)S(1)}, u32[]{:S(2)}, u32[]{:S(2)}) collective-permute-start(bf16[4,128,256]{2,1,0:T(8,128)(2,1)S(1)} %get-tuple-element.42), channel_id=1, source_target_pairs={{0,1},{1,0},{2,3},{3,2},{4,5},{5,4},{6,7},{7,6},{8,9},{9,8},{10,11... | collective-permute-start | bytes 786440 | tf_op jit(solution)/shard_map/ppermute | solution.py:29
  96.3 7.6 %collective-permute-start.17 = (bf16[3,128,256]{2,1,0:T(8,128)(2,1)S(1)}, bf16[3,128,256]{2,1,0:T(8,128)(2,1)S(1)}, u32[]{:S(2)}, u32[]{:S(2)}) collective-permute-start(bf16[3,128,256]{2,1,0:T(8,128)(2,1)S(1)} %get-tuple-element.43), channel_id=1, source_target_pairs={{0,1},{1,0},{2,3},{3,2},{4,5},{5,4},{6,7},{7,6},{8,9},{9,8},{10,11... | collective-permute-start | bytes 589832 | tf_op jit(solution)/shard_map/ppermute | solution.py:29

commit v4 on v3

--- a/solution.py
+++ b/solution.py
@@ -186,7 +186,7 @@
     ring, back, mine, other = {0: pack(earlier, earlier_other, received, received_other)}, (), [], []
     for step in range(1, NZ // 2 + 1):
         if step == 2:
-            ring[-1], ring[1], keep, send = lax.optimization_barrier((ring[-1], ring[1], keep, send))
+            ring[1], keep, send = lax.optimization_barrier((ring[1], keep, send))
             got = along(send, partner)
         if step == 5:
             one, two, *back = products(EARLY[0], False, place, (keep, got, *(ring[p] for p in EARLY[0])))

time: 107 us -> 107 us (level)
  starting transfers between devices: 67.8 us -> 69.3 us
  waiting for transfers between devices: 25.9 us -> 24.5 us
    ppermute x16, starting transfers between devices: 63.6 us -> 65.1 us  [along(): return lax.ppermute(block, 'fsdp', route)]
    ppermute x16, waiting for transfers between devices: 23 us -> 21.5 us  [along(): return lax.ppermute(block, 'fsdp', route)]
where the time goes in v4:
time: 107 us
  starting transfers between devices  69.3 us (65%)
  waiting for transfers between devices  24.5 us (23%)
  Pallas kernels  6.81 us (6%)
  local copies, waits for them, and re-layouts  4.4 us (4%)
  between operations  1.56 us (1%)
    ppermute x16, starting transfers between devices, along(): return lax.ppermute(block, 'fsdp', route)  65.1 us
    ppermute x16, waiting for transfers between devices, along(): return lax.ppermute(block, 'fsdp', route)  21.5 us
    pallas_call x5, Pallas kernels, call(): pl.pallas_call(kernel, out_shape=outs, in_specs=[scalar] * len(scalars) +...  6.77 us
    unnamed x10, local copies, waits for them, and re-layouts  4.4 us
    ppermute x2, starting transfers between devices, from_next_section(): return lax.ppermute(block, ('section', 'fsdp'), route)  4.25 us
    ppermute x2, waiting for transfers between devices, from_next_section(): return lax.ppermute(block, ('section', 'fsdp'), route)  2.92 us
  transfers between devices with their start and end apart: 18, of which 10 were waited for; matrix products, arithmetic and copies ran while one was open for 1% of the time, Pallas kernels for 4%

profile of v4, /device:TPU:6, one launch (start us, length us, event | category | flops | bytes accessed | tf_op | source)
XLA Modules:
  0.0 106.6 jit_solution(16337012512517184083)
XLA Ops:
  0.6 2.2 %collective-permute-start = (bf16[256,128]{1,0:T(8,128)(2,1)}, bf16[256,128]{1,0:T(8,128)(2,1)S(1)}, u32[]{:S(2)}, u32[]{:S(2)}) collective-permute-start(bf16[256,128]{1,0:T(8,128)(2,1)} %bitcast.14), channel_id=1, source_target_pairs={{48,0},{49,1},{50,2},{51,3},{52,4},{53,5},{54,6},{55,7},{56,8},{57... | collective-permute-start | bytes 196616 | tf_op jit(solution)/shard_map/ppermute | solution.py:39
  2.8 4.5 %collective-permute-start.1 = (bf16[256,128]{1,0:T(8,128)(2,1)}, bf16[256,128]{1,0:T(8,128)(2,1)S(1)}, u32[]{:S(2)}, u32[]{:S(2)}) collective-permute-start(bf16[256,128]{1,0:T(8,128)(2,1)} %bitcast.11), channel_id=1, source_target_pairs={{0,2},{1,3},{2,0},{3,1},{4,6},{5,7},{6,4},{7,5},{8,10},{9,11},{10,... | collective-permute-start | bytes 196616 | tf_op jit(solution)/shard_map/ppermute | solution.py:29
  7.3 2.1 %collective-permute-start.2 = (bf16[256,128]{1,0:T(8,128)(2,1)}, bf16[256,128]{1,0:T(8,128)(2,1)S(1)}, u32[]{:S(2)}, u32[]{:S(2)}) collective-permute-start(bf16[256,128]{1,0:T(8,128)(2,1)} %bitcast.15), channel_id=1, source_target_pairs={{50,0},{51,1},{48,2},{49,3},{54,4},{55,5},{52,6},{53,7},{58,8},{59... | collective-permute-start | bytes 196616 | tf_op jit(solution)/shard_map/ppermute | solution.py:39
  9.4 0.0 collective-permute-done.refs_2_.received_ref
  9.4 2.1 %collective-permute-done.1.refs_1_ = bf16[256,128]{1,0:T(8,128)(2,1)S(1)} collective-permute-done((bf16[256,128]{1,0:T(8,128)(2,1)}, bf16[256,128]{1,0:T(8,128)(2,1)S(1)}, u32[]{:S(2)}, u32[]{:S(2)}) %collective-permute-start.1) | collective-permute-done | bytes 65568 | tf_op jit(solution)/shard_map/ppermute | solution.py:29
  11.5 2.9 %collective-permute-done.2.refs_3_ = bf16[256,128]{1,0:T(8,128)(2,1)S(1)} collective-permute-done((bf16[256,128]{1,0:T(8,128)(2,1)}, bf16[256,128]{1,0:T(8,128)(2,1)S(1)}, u32[]{:S(2)}, u32[]{:S(2)}) %collective-permute-start.2) | collective-permute-done | bytes 65568 | tf_op jit(solution)/shard_map/ppermute | solution.py:39
  14.4 0.8 copy-done.3
  15.3 14.6 %collective-permute-start.3 = (bf16[512,256]{1,0:T(8,128)(2,1)S(1)}, bf16[512,256]{1,0:T(8,128)(2,1)S(1)}, u32[]{:S(2)}, u32[]{:S(2)}) collective-permute-start(bf16[512,256]{1,0:T(8,128)(2,1)S(1)} %pack.1.refs_0_), channel_id=1, source_target_pairs={{0,44},{1,45},{2,46},{3,47},{4,0},{5,1},{6,2},{7,3},{8,4},{9,5},{1... | collective-permute-start | bytes 786440 | tf_op jit(solution)/shard_map/ppermute | solution.py:29
  29.9 1.9 %collective-permute-start.5 = (bf16[512,256]{1,0:T(8,128)(2,1)S(1)}, bf16[512,256]{1,0:T(8,128)(2,1)S(1)}, u32[]{:S(2)}, u32[]{:S(2)}) collective-permute-start(bf16[512,256]{1,0:T(8,128)(2,1)S(1)} %pack.1.refs_0_), channel_id=1, source_target_pairs={{0,4},{1,5},{2,6},{3,7},{4,8},{5,9},{6,10},{7,11},{8,12},{9,13},{1... | collective-permute-start | bytes 786440 | tf_op jit(solution)/shard_map/ppermute | solution.py:29
  31.8 0.1 pad_add_fusion.place_ref
  31.9 0.7 copy.10.taps_ref
  33.2 0.0 copy-start
  33.3 1.4 %copy-done = bf16[1,128,6144]{2,1,0:T(8,128)(2,1)S(1)} copy-done((bf16[1,128,6144]{2,1,0:T(8,128)(2,1)S(1)}, bf16[1,128,6144]{2,1,0:T(8,128)(2,1)}, u32[]{:S(2)}) %copy-start) | copy-done | bytes 1572888
  34.7 0.9 copy-done.1
  35.6 1.2 %prepare.1 = (bf16[14,128,256]{2,1,0:T(8,128)(2,1)S(1)}, bf16[14,128,256]{2,1,0:T(8,128)(2,1)S(1)}) custom-call(s32[2]{0:T(128)S(1)} %pad_add_fusion.place_ref, s32[1]{0:T(128)S(6)} %copy.12.spacing_ref, bf16[2,256,128]{2,1,0:T(8,128)(2,1)S(1)} %bitcast.9, f32[1,3,128]{2,1,0:T(4,128)S(1)} %copy.10.taps_ref, bf16[128,6144]{1,0:T(8,128)(2,1)S(1)} %bitcast.8), custom_call_target="tpu_custom_call" | custom-call | bytes 1048576 | tf_op jit(solution)/shard_map/prepare/pallas_call | solution.py:99
  36.7 0.0 collective-permute-done.3.refs_2_
  36.8 3.6 %collective-permute-start.4 = (bf16[14,128,256]{2,1,0:T(8,128)(2,1)S(1)}, bf16[14,128,256]{2,1,0:T(8,128)(2,1)S(1)}, u32[]{:S(2)}, u32[]{:S(2)}) collective-permute-start(bf16[14,128,256]{2,1,0:T(8,128)(2,1)S(1)} %get-tuple-element.27), channel_id=1, source_target_pairs={{0,1},{1,0},{2,3},{3,2},{4,5},{5,4},{6,7},{7,6},{8,9},{9,8},{10,11... | collective-permute-start | bytes 2752520 | tf_op jit(solution)/shard_map/ppermute | solution.py:29
  40.3 0.0 collective-permute-done.5.refs_1_
  40.3 1.9 %collective-permute-start.6 = (bf16[512,256]{1,0:T(8,128)(2,1)S(1)}, bf16[512,256]{1,0:T(8,128)(2,1)S(1)}, u32[]{:S(2)}, u32[]{:S(2)}) collective-permute-start(bf16[512,256]{1,0:T(8,128)(2,1)S(1)} %collective-permute-done.5.refs_1_), channel_id=1, source_target_pairs={{0,4},{1,5},{2,6},{3,7},{4,8},{5,9},{6,10},{7,11},{8,12},{9,13},{1... | collective-permute-start | bytes 786440 | tf_op jit(solution)/shard_map/ppermute | solution.py:29
  42.3 5.1 %collective-permute-start.9 = (bf16[512,256]{1,0:T(8,128)(2,1)S(1)}, bf16[512,256]{1,0:T(8,128)(2,1)S(1)}, u32[]{:S(2)}, u32[]{:S(2)}) collective-permute-start(bf16[512,256]{1,0:T(8,128)(2,1)S(1)} %collective-permute-done.3.refs_2_), channel_id=1, source_target_pairs={{0,44},{1,45},{2,46},{3,47},{4,0},{5,1},{6,2},{7,3},{8,4},{9,5},{1... | collective-permute-start | bytes 786440 | tf_op jit(solution)/shard_map/ppermute | solution.py:29
  47.4 3.3 %collective-permute-done.6.refs_3_ = bf16[512,256]{1,0:T(8,128)(2,1)S(1)} collective-permute-done((bf16[512,256]{1,0:T(8,128)(2,1)S(1)}, bf16[512,256]{1,0:T(8,128)(2,1)S(1)}, u32[]{:S(2)}, u32[]{:S(2)}) %collective-permute-start.6) | collective-permute-done | bytes 262176 | tf_op jit(solution)/shard_map/ppermute | solution.py:29
  50.7 1.9 %collective-permute-start.7 = (bf16[512,256]{1,0:T(8,128)(2,1)S(1)}, bf16[512,256]{1,0:T(8,128)(2,1)S(1)}, u32[]{:S(2)}, u32[]{:S(2)}) collective-permute-start(bf16[512,256]{1,0:T(8,128)(2,1)S(1)} %collective-permute-done.6.refs_3_), channel_id=1, source_target_pairs={{0,4},{1,5},{2,6},{3,7},{4,8},{5,9},{6,10},{7,11},{8,12},{9,13},{1... | collective-permute-start | bytes 786440 | tf_op jit(solution)/shard_map/ppermute | solution.py:29
  52.6 0.0 collective-permute-done.9.refs_4_
  52.6 5.4 %collective-permute-start.10 = (bf16[512,256]{1,0:T(8,128)(2,1)S(1)}, bf16[512,256]{1,0:T(8,128)(2,1)S(1)}, u32[]{:S(2)}, u32[]{:S(2)}) collective-permute-start(bf16[512,256]{1,0:T(8,128)(2,1)S(1)} %collective-permute-done.9.refs_4_), channel_id=1, source_target_pairs={{0,44},{1,45},{2,46},{3,47},{4,0},{5,1},{6,2},{7,3},{8,4},{9,5},{1... | collective-permute-start | bytes 786440 | tf_op jit(solution)/shard_map/ppermute | solution.py:29
  58.0 4.2 %collective-permute-done.7.refs_5_ = bf16[512,256]{1,0:T(8,128)(2,1)S(1)} collective-permute-done((bf16[512,256]{1,0:T(8,128)(2,1)S(1)}, bf16[512,256]{1,0:T(8,128)(2,1)S(1)}, u32[]{:S(2)}, u32[]{:S(2)}) %collective-permute-start.7) | collective-permute-done | bytes 262176 | tf_op jit(solution)/shard_map/ppermute | solution.py:29
  62.2 1.9 %collective-permute-start.8 = (bf16[512,256]{1,0:T(8,128)(2,1)S(1)}, bf16[512,256]{1,0:T(8,128)(2,1)S(1)}, u32[]{:S(2)}, u32[]{:S(2)}) collective-permute-start(bf16[512,256]{1,0:T(8,128)(2,1)S(1)} %collective-permute-done.7.refs_5_), channel_id=1, source_target_pairs={{0,4},{1,5},{2,6},{3,7},{4,8},{5,9},{6,10},{7,11},{8,12},{9,13},{1... | collective-permute-start | bytes 786440 | tf_op jit(solution)/shard_map/ppermute | solution.py:29
  64.1 0.1 collective-permute-done.10.refs_6_
  64.3 5.6 %collective-permute-start.14 = (bf16[512,256]{1,0:T(8,128)(2,1)S(1)}, bf16[512,256]{1,0:T(8,128)(2,1)S(1)}, u32[]{:S(2)}, u32[]{:S(2)}) collective-permute-start(bf16[512,256]{1,0:T(8,128)(2,1)S(1)} %collective-permute-done.10.refs_6_), channel_id=1, source_target_pairs={{0,44},{1,45},{2,46},{3,47},{4,0},{5,1},{6,2},{7,3},{8,4},{9,5},{1... | collective-permute-start | bytes 786440 | tf_op jit(solution)/shard_map/ppermute | solution.py:29
  69.9 0.0 collective-permute-done.4.got_ref
  69.9 1.4 %products.3 = (bf16[7,128,256]{2,1,0:T(8,128)(2,1)S(1)}, bf16[7,128,256]{2,1,0:T(8,128)(2,1)S(1)}, f32[256,256]{1,0:T(8,128)S(1)}) custom-call(s32[2]{0:T(128)S(1)} %pad_add_fusion.place_ref, bf16[14,128,256]{2,1,0:T(8,128)(2,1)S(1)} %get-tuple-element.26.keep_ref, bf16[14,128,256]{2,1,0:T(8,128)(2,1)S(1)} %collective-permute-done.4.got_ref, ...), custom_call_target="tpu_custom_call" | custom-call | flops 939524096 | bytes 1048576 | tf_op jit(solution)/shard_map/products/pallas_call | solution.py:99
  71.3 2.8 %collective-permute-done.8.refs_0_ = bf16[512,256]{1,0:T(8,128)(2,1)S(1)} collective-permute-done((bf16[512,256]{1,0:T(8,128)(2,1)S(1)}, bf16[512,256]{1,0:T(8,128)(2,1)S(1)}, u32[]{:S(2)}, u32[]{:S(2)}) %collective-permute-start.8) | collective-permute-done | bytes 262176 | tf_op jit(solution)/shard_map/ppermute | solution.py:29
  74.1 1.9 %collective-permute-start.11 = (bf16[512,256]{1,0:T(8,128)(2,1)S(1)}, bf16[512,256]{1,0:T(8,128)(2,1)S(1)}, u32[]{:S(2)}, u32[]{:S(2)}) collective-permute-start(bf16[512,256]{1,0:T(8,128)(2,1)S(1)} %collective-permute-done.8.refs_0_), channel_id=1, source_target_pairs={{0,4},{1,5},{2,6},{3,7},{4,8},{5,9},{6,10},{7,11},{8,12},{9,13},{1... | collective-permute-start | bytes 786440 | tf_op jit(solution)/shard_map/ppermute | solution.py:29
  76.0 4.2 %collective-permute-start.13 = (bf16[7,128,256]{2,1,0:T(8,128)(2,1)S(1)}, bf16[7,128,256]{2,1,0:T(8,128)(2,1)S(1)}, u32[]{:S(2)}, u32[]{:S(2)}) collective-permute-start(bf16[7,128,256]{2,1,0:T(8,128)(2,1)S(1)} %get-tuple-element.31), channel_id=1, source_target_pairs={{0,1},{1,0},{2,3},{3,2},{4,5},{5,4},{6,7},{7,6},{8,9},{9,8},{10,11... | collective-permute-start | bytes 1376264 | tf_op jit(solution)/shard_map/ppermute | solution.py:29
  80.3 0.0 collective-permute-done.14.refs_1_
  80.3 5.1 %collective-permute-start.15 = (bf16[512,256]{1,0:T(8,128)(2,1)S(1)}, bf16[512,256]{1,0:T(8,128)(2,1)S(1)}, u32[]{:S(2)}, u32[]{:S(2)}) collective-permute-start(bf16[512,256]{1,0:T(8,128)(2,1)S(1)} %collective-permute-done.14.refs_1_), channel_id=1, source_target_pairs={{0,44},{1,45},{2,46},{3,47},{4,0},{5,1},{6,2},{7,3},{8,4},{9,5},{1... | collective-permute-start | bytes 786440 | tf_op jit(solution)/shard_map/ppermute | solution.py:29
  85.4 0.0 collective-permute-done.11.refs_2_
  85.4 1.9 %collective-permute-start.12 = (bf16[512,256]{1,0:T(8,128)(2,1)S(1)}, bf16[512,256]{1,0:T(8,128)(2,1)S(1)}, u32[]{:S(2)}, u32[]{:S(2)}) collective-permute-start(bf16[512,256]{1,0:T(8,128)(2,1)S(1)} %collective-permute-done.11.refs_2_), channel_id=1, source_target_pairs={{0,4},{1,5},{2,6},{3,7},{4,8},{5,9},{6,10},{7,11},{8,12},{9,13},{1... | collective-permute-start | bytes 786440 | tf_op jit(solution)/shard_map/ppermute | solution.py:29
  87.3 2.5 %collective-permute-done.15.refs_3_ = bf16[512,256]{1,0:T(8,128)(2,1)S(1)} collective-permute-done((bf16[512,256]{1,0:T(8,128)(2,1)S(1)}, bf16[512,256]{1,0:T(8,128)(2,1)S(1)}, u32[]{:S(2)}, u32[]{:S(2)}) %collective-permute-start.15) | collective-permute-done | bytes 262176 | tf_op jit(solution)/shard_map/ppermute | solution.py:29
  89.8 1.1 %products.4 = (bf16[4,128,256]{2,1,0:T(8,128)(2,1)S(1)}, bf16[4,128,256]{2,1,0:T(8,128)(2,1)S(1)}, f32[256,256]{1,0:T(8,128)S(1)}) custom-call(s32[2]{0:T(128)S(1)} %pad_add_fusion.place_ref, bf16[14,128,256]{2,1,0:T(8,128)(2,1)S(1)} %get-tuple-element.26.keep_ref, bf16[14,128,256]{2,1,0:T(8,128)(2,1)S(1)} %collective-permute-done.4.got_ref, ...), custom_call_target="tpu_custom_call" | custom-call | flops 536870912 | bytes 1048576 | tf_op jit(solution)/shard_map/products/pallas_call | solution.py:99
  90.9 0.0 copy-start.2
  91.0 2.3 %collective-permute-start.16 = (bf16[4,128,256]{2,1,0:T(8,128)(2,1)S(1)}, bf16[4,128,256]{2,1,0:T(8,128)(2,1)S(1)}, u32[]{:S(2)}, u32[]{:S(2)}) collective-permute-start(bf16[4,128,256]{2,1,0:T(8,128)(2,1)S(1)} %get-tuple-element.40), channel_id=1, source_target_pairs={{0,1},{1,0},{2,3},{3,2},{4,5},{5,4},{6,7},{7,6},{8,9},{9,8},{10,11... | collective-permute-start | bytes 786440 | tf_op jit(solution)/shard_map/ppermute | solution.py:29
  93.3 2.1 %collective-permute-done.12.refs_0_ = bf16[512,256]{1,0:T(8,128)(2,1)S(1)} collective-permute-done((bf16[512,256]{1,0:T(8,128)(2,1)S(1)}, bf16[512,256]{1,0:T(8,128)(2,1)S(1)}, u32[]{:S(2)}, u32[]{:S(2)}) %collective-permute-start.12) | collective-permute-done | bytes 262176 | tf_op jit(solution)/shard_map/ppermute | solution.py:29
  95.4 0.8 products.5
  96.3 3.1 %collective-permute-start.17 = (bf16[3,128,256]{2,1,0:T(8,128)(2,1)S(1)}, bf16[3,128,256]{2,1,0:T(8,128)(2,1)S(1)}, u32[]{:S(2)}, u32[]{:S(2)}) collective-permute-start(bf16[3,128,256]{2,1,0:T(8,128)(2,1)S(1)} %get-tuple-element.41), channel_id=1, source_target_pairs={{0,1},{1,0},{2,3},{3,2},{4,5},{5,4},{6,7},{7,6},{8,9},{9,8},{10,11... | collective-permute-start | bytes 589832 | tf_op jit(solution)/shard_map/ppermute | solution.py:29
  99.4 0.7 collective-permute-done.16.refs_4_
  100.1 3.8 %collective-permute-done.17.refs_5_ = bf16[3,128,256]{2,1,0:T(8,128)(2,1)S(1)} collective-permute-done((bf16[3,128,256]{2,1,0:T(8,128)(2,1)S(1)}, bf16[3,128,256]{2,1,0:T(8,128)(2,1)S(1)}, u32[]{:S(2)}, u32[]{:S(2)}) %collective-permute-start.17) | collective-permute-done | bytes 196640 | tf_op jit(solution)/shard_map/ppermute | solution.py:29
  103.8 2.2 %finish.1 = (bf16[256,128]{1,0:T(8,128)(2,1)}, f32[1,3,128]{2,1,0:T(4,128)S(1)}, bf16[128,6144]{1,0:T(8,128)(2,1)}) custom-call(s32[2]{0:T(128)S(1)} %pad_add_fusion.place_ref, s32[1]{0:T(128)S(6)} %copy.12.spacing_ref, bf16[256,128]{1,0:T(8,128)(2,1)S(1)} %collective-permute-done.refs_2_.received_ref, bf16[2,256,128]{2,1,0:T(8,128)(2,1)S(1)} %bitcast.10, ...), custom_call_target="tpu_custom_call" | custom-call | bytes 1048576 | tf_op jit(solution)/shard_map/finish/pallas_call | solution.py:99
  106.0 0.6 copy.11
  (5 shorter events, 0.1 us)
Async XLA Ops:
  0.6 8.8 %collective-permute-start = (bf16[256,128]{1,0:T(8,128)(2,1)}, bf16[256,128]{1,0:T(8,128)(2,1)S(1)}, u32[]{:S(2)}, u32[]{:S(2)}) collective-permute-start(bf16[256,128]{1,0:T(8,128)(2,1)} %bitcast.14), channel_id=1, source_target_pairs={{48,0},{49,1},{50,2},{51,3},{52,4},{53,5},{54,6},{55,7},{56,8},{57... | collective-permute-start | bytes 196616 | tf_op jit(solution)/shard_map/ppermute | solution.py:39
  2.8 8.7 %collective-permute-start.1 = (bf16[256,128]{1,0:T(8,128)(2,1)}, bf16[256,128]{1,0:T(8,128)(2,1)S(1)}, u32[]{:S(2)}, u32[]{:S(2)}) collective-permute-start(bf16[256,128]{1,0:T(8,128)(2,1)} %bitcast.11), channel_id=1, source_target_pairs={{0,2},{1,3},{2,0},{3,1},{4,6},{5,7},{6,4},{7,5},{8,10},{9,11},{10,... | collective-permute-start | bytes 196616 | tf_op jit(solution)/shard_map/ppermute | solution.py:29
  7.3 7.1 %collective-permute-start.2 = (bf16[256,128]{1,0:T(8,128)(2,1)}, bf16[256,128]{1,0:T(8,128)(2,1)S(1)}, u32[]{:S(2)}, u32[]{:S(2)}) collective-permute-start(bf16[256,128]{1,0:T(8,128)(2,1)} %bitcast.15), channel_id=1, source_target_pairs={{50,0},{51,1},{48,2},{49,3},{54,4},{55,5},{52,6},{53,7},{58,8},{59... | collective-permute-start | bytes 196616 | tf_op jit(solution)/shard_map/ppermute | solution.py:39
  14.4 0.8 copy-start.3
  15.3 21.5 %collective-permute-start.3 = (bf16[512,256]{1,0:T(8,128)(2,1)S(1)}, bf16[512,256]{1,0:T(8,128)(2,1)S(1)}, u32[]{:S(2)}, u32[]{:S(2)}) collective-permute-start(bf16[512,256]{1,0:T(8,128)(2,1)S(1)} %pack.1.refs_0_), channel_id=1, source_target_pairs={{0,44},{1,45},{2,46},{3,47},{4,0},{5,1},{6,2},{7,3},{8,4},{9,5},{1... | collective-permute-start | bytes 786440 | tf_op jit(solution)/shard_map/ppermute | solution.py:29
  29.9 10.4 %collective-permute-start.5 = (bf16[512,256]{1,0:T(8,128)(2,1)S(1)}, bf16[512,256]{1,0:T(8,128)(2,1)S(1)}, u32[]{:S(2)}, u32[]{:S(2)}) collective-permute-start(bf16[512,256]{1,0:T(8,128)(2,1)S(1)} %pack.1.refs_0_), channel_id=1, source_target_pairs={{0,4},{1,5},{2,6},{3,7},{4,8},{5,9},{6,10},{7,11},{8,12},{9,13},{1... | collective-permute-start | bytes 786440 | tf_op jit(solution)/shard_map/ppermute | solution.py:29
  33.2 1.4 %copy-start = (bf16[1,128,6144]{2,1,0:T(8,128)(2,1)S(1)}, bf16[1,128,6144]{2,1,0:T(8,128)(2,1)}, u32[]{:S(2)}) copy-start(bf16[1,128,6144]{2,1,0:T(8,128)(2,1)} %param.9) | copy-start | bytes 4718596
  34.7 0.9 copy-start.1
  36.8 33.1 %collective-permute-start.4 = (bf16[14,128,256]{2,1,0:T(8,128)(2,1)S(1)}, bf16[14,128,256]{2,1,0:T(8,128)(2,1)S(1)}, u32[]{:S(2)}, u32[]{:S(2)}) collective-permute-start(bf16[14,128,256]{2,1,0:T(8,128)(2,1)S(1)} %get-tuple-element.27), channel_id=1, source_target_pairs={{0,1},{1,0},{2,3},{3,2},{4,5},{5,4},{6,7},{7,6},{8,9},{9,8},{10,11... | collective-permute-start | bytes 2752520 | tf_op jit(solution)/shard_map/ppermute | solution.py:29
  40.3 10.3 %collective-permute-start.6 = (bf16[512,256]{1,0:T(8,128)(2,1)S(1)}, bf16[512,256]{1,0:T(8,128)(2,1)S(1)}, u32[]{:S(2)}, u32[]{:S(2)}) collective-permute-start(bf16[512,256]{1,0:T(8,128)(2,1)S(1)} %collective-permute-done.5.refs_1_), channel_id=1, source_target_pairs={{0,4},{1,5},{2,6},{3,7},{4,8},{5,9},{6,10},{7,11},{8,12},{9,13},{1... | collective-permute-start | bytes 786440 | tf_op jit(solution)/shard_map/ppermute | solution.py:29
  42.3 10.3 %collective-permute-start.9 = (bf16[512,256]{1,0:T(8,128)(2,1)S(1)}, bf16[512,256]{1,0:T(8,128)(2,1)S(1)}, u32[]{:S(2)}, u32[]{:S(2)}) collective-permute-start(bf16[512,256]{1,0:T(8,128)(2,1)S(1)} %collective-permute-done.3.refs_2_), channel_id=1, source_target_pairs={{0,44},{1,45},{2,46},{3,47},{4,0},{5,1},{6,2},{7,3},{8,4},{9,5},{1... | collective-permute-start | bytes 786440 | tf_op jit(solution)/shard_map/ppermute | solution.py:29
  50.7 11.5 %collective-permute-start.7 = (bf16[512,256]{1,0:T(8,128)(2,1)S(1)}, bf16[512,256]{1,0:T(8,128)(2,1)S(1)}, u32[]{:S(2)}, u32[]{:S(2)}) collective-permute-start(bf16[512,256]{1,0:T(8,128)(2,1)S(1)} %collective-permute-done.6.refs_3_), channel_id=1, source_target_pairs={{0,4},{1,5},{2,6},{3,7},{4,8},{5,9},{6,10},{7,11},{8,12},{9,13},{1... | collective-permute-start | bytes 786440 | tf_op jit(solution)/shard_map/ppermute | solution.py:29
  52.6 11.6 %collective-permute-start.10 = (bf16[512,256]{1,0:T(8,128)(2,1)S(1)}, bf16[512,256]{1,0:T(8,128)(2,1)S(1)}, u32[]{:S(2)}, u32[]{:S(2)}) collective-permute-start(bf16[512,256]{1,0:T(8,128)(2,1)S(1)} %collective-permute-done.9.refs_4_), channel_id=1, source_target_pairs={{0,44},{1,45},{2,46},{3,47},{4,0},{5,1},{6,2},{7,3},{8,4},{9,5},{1... | collective-permute-start | bytes 786440 | tf_op jit(solution)/shard_map/ppermute | solution.py:29
  62.2 11.9 %collective-permute-start.8 = (bf16[512,256]{1,0:T(8,128)(2,1)S(1)}, bf16[512,256]{1,0:T(8,128)(2,1)S(1)}, u32[]{:S(2)}, u32[]{:S(2)}) collective-permute-start(bf16[512,256]{1,0:T(8,128)(2,1)S(1)} %collective-permute-done.7.refs_5_), channel_id=1, source_target_pairs={{0,4},{1,5},{2,6},{3,7},{4,8},{5,9},{6,10},{7,11},{8,12},{9,13},{1... | collective-permute-start | bytes 786440 | tf_op jit(solution)/shard_map/ppermute | solution.py:29
  64.3 16.0 %collective-permute-start.14 = (bf16[512,256]{1,0:T(8,128)(2,1)S(1)}, bf16[512,256]{1,0:T(8,128)(2,1)S(1)}, u32[]{:S(2)}, u32[]{:S(2)}) collective-permute-start(bf16[512,256]{1,0:T(8,128)(2,1)S(1)} %collective-permute-done.10.refs_6_), channel_id=1, source_target_pairs={{0,44},{1,45},{2,46},{3,47},{4,0},{5,1},{6,2},{7,3},{8,4},{9,5},{1... | collective-permute-start | bytes 786440 | tf_op jit(solution)/shard_map/ppermute | solution.py:29
  74.1 11.3 %collective-permute-start.11 = (bf16[512,256]{1,0:T(8,128)(2,1)S(1)}, bf16[512,256]{1,0:T(8,128)(2,1)S(1)}, u32[]{:S(2)}, u32[]{:S(2)}) collective-permute-start(bf16[512,256]{1,0:T(8,128)(2,1)S(1)} %collective-permute-done.8.refs_0_), channel_id=1, source_target_pairs={{0,4},{1,5},{2,6},{3,7},{4,8},{5,9},{6,10},{7,11},{8,12},{9,13},{1... | collective-permute-start | bytes 786440 | tf_op jit(solution)/shard_map/ppermute | solution.py:29
  76.0 17.3 %collective-permute-start.13 = (bf16[7,128,256]{2,1,0:T(8,128)(2,1)S(1)}, bf16[7,128,256]{2,1,0:T(8,128)(2,1)S(1)}, u32[]{:S(2)}, u32[]{:S(2)}) collective-permute-start(bf16[7,128,256]{2,1,0:T(8,128)(2,1)S(1)} %get-tuple-element.31), channel_id=1, source_target_pairs={{0,1},{1,0},{2,3},{3,2},{4,5},{5,4},{6,7},{7,6},{8,9},{9,8},{10,11... | collective-permute-start | bytes 1376264 | tf_op jit(solution)/shard_map/ppermute | solution.py:29
  80.3 9.5 %collective-permute-start.15 = (bf16[512,256]{1,0:T(8,128)(2,1)S(1)}, bf16[512,256]{1,0:T(8,128)(2,1)S(1)}, u32[]{:S(2)}, u32[]{:S(2)}) collective-permute-start(bf16[512,256]{1,0:T(8,128)(2,1)S(1)} %collective-permute-done.14.refs_1_), channel_id=1, source_target_pairs={{0,44},{1,45},{2,46},{3,47},{4,0},{5,1},{6,2},{7,3},{8,4},{9,5},{1... | collective-permute-start | bytes 786440 | tf_op jit(solution)/shard_map/ppermute | solution.py:29
  85.4 10.0 %collective-permute-start.12 = (bf16[512,256]{1,0:T(8,128)(2,1)S(1)}, bf16[512,256]{1,0:T(8,128)(2,1)S(1)}, u32[]{:S(2)}, u32[]{:S(2)}) collective-permute-start(bf16[512,256]{1,0:T(8,128)(2,1)S(1)} %collective-permute-done.11.refs_2_), channel_id=1, source_target_pairs={{0,4},{1,5},{2,6},{3,7},{4,8},{5,9},{6,10},{7,11},{8,12},{9,13},{1... | collective-permute-start | bytes 786440 | tf_op jit(solution)/shard_map/ppermute | solution.py:29
  90.9 12.9 %copy-start.2 = (bf16[1,2,256,128]{3,2,1,0:T(8,128)(2,1)S(1)}, bf16[1,2,256,128]{3,2,1,0:T(8,128)(2,1)}, u32[]{:S(2)}) copy-start(bf16[1,2,256,128]{3,2,1,0:T(8,128)(2,1)} %param.6) | copy-start | bytes 393220
  91.0 9.1 %collective-permute-start.16 = (bf16[4,128,256]{2,1,0:T(8,128)(2,1)S(1)}, bf16[4,128,256]{2,1,0:T(8,128)(2,1)S(1)}, u32[]{:S(2)}, u32[]{:S(2)}) collective-permute-start(bf16[4,128,256]{2,1,0:T(8,128)(2,1)S(1)} %get-tuple-element.40), channel_id=1, source_target_pairs={{0,1},{1,0},{2,3},{3,2},{4,5},{5,4},{6,7},{7,6},{8,9},{9,8},{10,11... | collective-permute-start | bytes 786440 | tf_op jit(solution)/shard_map/ppermute | solution.py:29
  96.3 7.6 %collective-permute-start.17 = (bf16[3,128,256]{2,1,0:T(8,128)(2,1)S(1)}, bf16[3,128,256]{2,1,0:T(8,128)(2,1)S(1)}, u32[]{:S(2)}, u32[]{:S(2)}) collective-permute-start(bf16[3,128,256]{2,1,0:T(8,128)(2,1)S(1)} %get-tuple-element.41), channel_id=1, source_target_pairs={{0,1},{1,0},{2,3},{3,2},{4,5},{5,4},{6,7},{7,6},{8,9},{9,8},{10,11... | collective-permute-start | bytes 589832 | tf_op jit(solution)/shard_map/ppermute | solution.py:29
